TPU v7x, 128 devices: a whole 4x4x4 slice. The times are simulated.
128 devices in a mesh: dp: 16 (over z, x_hi, core), ctx: 8 (over x_lo, y).
Axes of the slice: x: 4 (x_hi: 2, x_lo: 2; x = x_hi * 2 + x_lo), y: 4, z: 4, core: 2. Of those that a mesh axis runs over, the one named last changes fastest.
Arguments:
- tokens: bfloat16 [16384, 2048], P(('dp', 'ctx')), may hold values from -6 to 6
- positions: int32 [16384], P(('dp', 'ctx')), may hold values from 0 to 1023, as said below
- attn_in: bfloat16 [2048, 2560], P(('dp', 'ctx')), may hold values from -0.125 to 0.125
- attn_out: bfloat16 [2048, 2048], P(('dp', 'ctx')), may hold values from -0.5 to 0.5
- attn_gain: bfloat16 [2048], P(('dp', 'ctx')), may hold values from 0.5 to 1.5
- mlp_in: bfloat16 [2048, 11264], P(('dp', 'ctx')), may hold values from -0.125 to 0.125
- mlp_down: bfloat16 [2048, 5632], P(('dp', 'ctx')), may hold values from -0.078125 to 0.078125
- mlp_gain: bfloat16 [2048], P(('dp', 'ctx')), may hold values from 0.5 to 1.5
- cotangent: bfloat16 [16384, 2048], P(('dp', 'ctx')), may hold values from -6 to 6
Outputs:
- activations: bfloat16 [16384, 2048], P(('dp', 'ctx'))
- input_grad: float32 [16384, 2048], P(('dp', 'ctx'))
- grad_attn_in: float32 [2048, 2560], P(('dp', 'ctx'))
- grad_attn_out: float32 [2048, 2048], P(('dp', 'ctx'))
- grad_attn_gain: float32 [2048], P(('dp', 'ctx'))
- grad_mlp_in: float32 [2048, 11264], P(('dp', 'ctx'))
- grad_mlp_down: float32 [2048, 5632], P(('dp', 'ctx'))
- grad_mlp_gain: float32 [2048], P(('dp', 'ctx'))
Inputs may be any that keep to these rules, and one draw needn't show every extreme that they name: Within each sequence positions rise by one from token to token and restart at 0 where a document begins; the first document of a sequence may continue one begun earlier. One document of every sequence begins within its first 128 tokens and ends within its last 128.
All inputs are finite; a program needn't handle non-finite values.
Results may differ from a plain program's by a relative error of at most 0.019.
Values may be sent and summed in bfloat16 or wider, within the bound.
A program may use at most 192 MiB of HBM per device.

v0:
```python
import math

import jax
import jax.numpy as jnp
from jax import lax
from jax.sharding import PartitionSpec as P

HEADS = 32
KV_HEADS = 4
HEAD_DIM = 64
FF = 5632


EPS = 1e-05
ROPE_BASE = 10000.0
NEG_FILL = -1e30


def in_one_piece(arrays, axis, dim, along):
    widths = [math.prod(a.shape[along:]) for a in arrays]
    both = jnp.concatenate(
        [a.reshape(*a.shape[:along], w) for a, w in zip(arrays, widths)], axis=along
    )
    out = lax.all_gather(both, axis, axis=dim, tiled=True)
    blocks = jnp.split(out, [sum(widths[:k]) for k in range(1, len(widths))], axis=along)
    return tuple((b.reshape(*out.shape[:along], *a.shape[along:]) for a, b in zip(arrays, blocks)))


def in_one_piece_2(arrays, axis, split_dim, concat_dim, along):
    both = jnp.concatenate(arrays, axis=along)
    out, at, outs = (
        lax.all_to_all(both, axis, split_axis=split_dim, concat_axis=concat_dim, tiled=True),
        0,
        [],
    )
    for a in arrays:
        outs.append(lax.slice_in_dim(out, at, at + a.shape[along], axis=along))
        at += a.shape[along]
    return tuple(outs)


def in_one_piece_3(arrays, axis, dim, along):
    ends, at = ([], 0)
    for a in arrays[:-1]:
        at += a.shape[along]
        ends.append(at)
    both = jnp.concatenate(arrays, axis=along)
    return tuple(jnp.split(lax.all_gather(both, axis, axis=dim, tiled=True), ends, axis=along))


def sent_together(arrays, axis, dim, along):
    ends, at = ([], 0)
    for a in arrays[:-1]:
        at += a.shape[along]
        ends.append(at)
    both = jnp.concatenate(arrays, axis=along)
    return tuple(
        jnp.split(lax.psum_scatter(both, axis, scatter_dimension=dim, tiled=True), ends, axis=along)
    )


def side_by_side(arrays, axis, dim, along):
    columns = [a.reshape(*a.shape[:along], -1) for a in arrays]
    both = jnp.concatenate(columns, axis=along)
    out, at, outs = (lax.psum_scatter(both, axis, scatter_dimension=dim, tiled=True), 0, [])
    for a, column in zip(arrays, columns):
        piece = out[..., at : at + column.shape[along]]
        outs.append(piece.reshape(*piece.shape[:along], *a.shape[along:]))
        at += column.shape[along]
    return tuple(outs)


def angles(positions, head_dim):
    inv_freq = ROPE_BASE ** (-jnp.arange(0, head_dim, 2, dtype=jnp.float32) / head_dim)
    phase_angle = positions.astype(jnp.float32)[:, None] * inv_freq[None, :]
    return (jnp.cos(phase_angle)[:, None, :], jnp.sin(phase_angle)[:, None, :])


def rotary(values, cosines, sines):
    half_dim = values.shape[-1] // 2
    first_half = values[..., :half_dim]
    second = values[..., half_dim:]
    return jnp.concatenate(
        [first_half * cosines - second * sines, second * cosines + first_half * sines], axis=-1
    )


def norm_parts(values, gain_vec):
    inv_root = lax.rsqrt(jnp.mean(values * values, -1, keepdims=True) + EPS)
    normed = values * inv_root
    return (inv_root, normed, normed * gain_vec)


def norm_back(grad_scaled, inv_root, normed, gain_vec):
    grad_normed = grad_scaled * gain_vec
    grad_values = inv_root * (
        grad_normed - normed * jnp.mean(grad_normed * normed, -1, keepdims=True)
    )
    return (grad_values, jnp.sum(grad_scaled * normed, 0))


def gather_attention(attn_in, attn_out, attn_gain, mlp_gain):
    return in_one_piece((attn_in, attn_out, attn_gain, mlp_gain), ("dp", "ctx"), 0, 1)


def fetch_hidden(mlp_in, mlp_down):
    rows_here = mlp_in.shape[0]
    width = mlp_down.shape[1]
    swapped_gu, swapped_down = in_one_piece_2(
        (mlp_in.reshape(rows_here, 2, width), mlp_down.reshape(rows_here, 1, width)), "ctx", 2, 0, 1
    )
    return in_one_piece_3((swapped_gu, swapped_down), "dp", 0, 1)


def contract_rows(left_mat, right_mat):
    return lax.dot_general(
        left_mat, right_mat, (((0,), (0,)), ((), ())), preferred_element_type=jnp.float32
    )


def contract_cols(left_mat, right_mat):
    return lax.dot_general(
        left_mat, right_mat, (((1,), (1,)), ((), ())), preferred_element_type=jnp.float32
    )


def shards(tokens, positions, attn_in, attn_out, attn_gain, mlp_in, mlp_down, mlp_gain, cotangent):
    row_count = tokens.shape[0]
    model_width = tokens.shape[1]
    head_dim = HEAD_DIM
    kv_heads = KV_HEADS
    repeat = HEADS // KV_HEADS
    kv_width = kv_heads * head_dim
    hidden = FF
    score_scale = head_dim ** (-0.5)
    inputs = tokens.astype(jnp.float32)
    weight_in, weight_out, gain_one, gain_two = gather_attention(
        attn_in, attn_out, attn_gain, mlp_gain
    )
    gain_one = gain_one.astype(jnp.float32)
    gain_two = gain_two.astype(jnp.float32)
    inv_one, normed_one, scaled = norm_parts(inputs, gain_one)
    scaled_one = scaled.astype(jnp.bfloat16)
    projected = jnp.dot(scaled_one, weight_in, preferred_element_type=jnp.float32)
    cosines, sines = angles(positions, head_dim)
    queries = rotary(projected[:, :model_width].reshape(row_count, HEADS, head_dim), cosines, sines)
    queries = queries.astype(jnp.bfloat16).reshape(row_count, kv_heads, repeat, head_dim)
    keys_local = rotary(
        projected[:, model_width : model_width + kv_width].reshape(row_count, kv_heads, head_dim),
        cosines,
        sines,
    )
    keys_local = keys_local.astype(jnp.bfloat16).reshape(row_count, kv_width)
    values_local = projected[:, model_width + kv_width :].astype(jnp.bfloat16)
    keys_all, values_all = in_one_piece_3((keys_local, values_local), "ctx", 0, 1)
    length = keys_all.shape[0]
    keys_all = keys_all.reshape(length, kv_heads, head_dim)
    values_all = values_all.reshape(length, kv_heads, head_dim)
    query_index = lax.axis_index("ctx") * row_count + jnp.arange(row_count, dtype=jnp.int32)
    key_index = jnp.arange(length, dtype=jnp.int32)
    visible = (key_index[None, :] <= query_index[:, None]) & (
        query_index[:, None] - key_index[None, :] <= positions[:, None]
    )

    def masked_scores():
        raw_scores = jnp.einsum(
            "qgrd,kgd->grqk", queries, keys_all, preferred_element_type=jnp.float32
        )
        return jnp.where(visible[None, None], raw_scores * score_scale, NEG_FILL)

    scores = masked_scores()
    row_peak = jnp.max(scores, -1, keepdims=True)
    scores_exp = jnp.exp(scores - row_peak)
    row_total = jnp.sum(scores_exp, -1, keepdims=True)
    probs_low = (scores_exp / row_total).astype(jnp.bfloat16)
    log_total = row_peak + jnp.log(row_total)
    attended = jnp.einsum(
        "grqk,kgd->qgrd", probs_low, values_all, preferred_element_type=jnp.float32
    )
    attended_low = attended.reshape(row_count, model_width).astype(jnp.bfloat16)
    middle = inputs + jnp.dot(attended_low, weight_out, preferred_element_type=jnp.float32)
    inv_two, normed_two, scaled = norm_parts(middle, gain_two)
    scaled_two = scaled.astype(jnp.bfloat16)
    grad_out = cotangent.astype(jnp.float32)
    seq_scaled = lax.all_gather(scaled_two, "ctx", axis=0, tiled=True)
    hidden_gu, hidden_down = fetch_hidden(mlp_in, mlp_down)
    gate_up = jnp.einsum("td,dkf->tkf", seq_scaled, hidden_gu, preferred_element_type=jnp.float32)
    gate_pre = gate_up[:, 0]
    up_pre = gate_up[:, 1]
    gate_sigmoid = jax.nn.sigmoid(gate_pre)
    gate_silu = gate_pre * gate_sigmoid
    hidden_act = (gate_silu * up_pre).astype(jnp.bfloat16)
    down_block = hidden_down[:, 0]
    outputs = middle + lax.psum_scatter(
        contract_cols(hidden_act, down_block).astype(jnp.bfloat16),
        "ctx",
        scatter_dimension=0,
        tiled=True,
    ).astype(jnp.float32)
    back_gu, back_down = fetch_hidden(mlp_in, mlp_down)
    seq_grad = lax.all_gather(cotangent, "ctx", axis=0, tiled=True)
    grad_hidden = jnp.dot(seq_grad, back_down[:, 0], preferred_element_type=jnp.float32)
    grad_gate = grad_hidden * up_pre * gate_sigmoid * (1.0 + gate_pre * (1.0 - gate_sigmoid))
    grad_up = grad_hidden * gate_silu
    grad_gu_low = jnp.stack([grad_gate, grad_up], 1).astype(jnp.bfloat16)
    grad_two = lax.psum_scatter(
        jnp.einsum("tkf,dkf->td", grad_gu_low, back_gu, preferred_element_type=jnp.float32).astype(
            jnp.bfloat16
        ),
        "ctx",
        scatter_dimension=0,
        tiled=True,
    ).astype(jnp.float32)
    grad_mid_norm, grad_gain_two = norm_back(grad_two, inv_two, normed_two, gain_two)
    grad_middle = grad_out + grad_mid_norm
    part_in = jnp.einsum("td,tkf->dkf", seq_scaled, grad_gu_low, preferred_element_type=jnp.float32)
    part_down = contract_rows(seq_grad, hidden_act)[:, None, :]
    summed = lax.psum_scatter(
        jnp.concatenate([part_in, part_down], 1).astype(jnp.bfloat16),
        "dp",
        scatter_dimension=0,
        tiled=True,
    ).astype(jnp.float32)
    owned = lax.all_to_all(
        summed.astype(jnp.bfloat16), "ctx", split_axis=0, concat_axis=2, tiled=True
    ).astype(summed.dtype)
    grad_mlp_in = owned[:, :2].reshape(mlp_in.shape[0], 2 * hidden)
    grad_mlp_down = owned[:, 2]
    back_in, back_out, back_gain_one, unused_gain = gather_attention(
        attn_in, attn_out, attn_gain, mlp_gain
    )
    back_gain_one = back_gain_one.astype(jnp.float32)
    grad_branch_low = grad_middle.astype(jnp.bfloat16)
    grad_att_low = contract_cols(grad_branch_low, back_out).astype(jnp.bfloat16)
    grad_att_heads = grad_att_low.reshape(row_count, kv_heads, repeat, head_dim)
    probs_again = jnp.exp(masked_scores() - log_total)
    grad_probs = jnp.einsum(
        "qgrd,kgd->grqk", grad_att_heads, values_all, preferred_element_type=jnp.float32
    )
    row_delta = jnp.sum(probs_again * grad_probs, -1, keepdims=True)
    grad_scores_low = (probs_again * (grad_probs - row_delta)).astype(jnp.bfloat16)
    grad_queries = (
        jnp.einsum("grqk,kgd->qgrd", grad_scores_low, keys_all, preferred_element_type=jnp.float32)
        * score_scale
    )
    grad_keys_all = (
        jnp.einsum("grqk,qgrd->kgd", grad_scores_low, queries, preferred_element_type=jnp.float32)
        * score_scale
    )
    grad_values_all = jnp.einsum(
        "grqk,qgrd->kgd",
        probs_again.astype(jnp.bfloat16),
        grad_att_heads,
        preferred_element_type=jnp.float32,
    )
    grad_keys, grad_values = tuple(
        (
            part.astype(jnp.float32)
            for part in sent_together(
                (
                    grad_keys_all.reshape(length, kv_width).astype(jnp.bfloat16),
                    grad_values_all.reshape(length, kv_width).astype(jnp.bfloat16),
                ),
                "ctx",
                0,
                1,
            )
        )
    )
    grad_q_raw = rotary(grad_queries.reshape(row_count, HEADS, head_dim), cosines, -sines).reshape(
        row_count, model_width
    )
    grad_k_raw = rotary(grad_keys.reshape(row_count, kv_heads, head_dim), cosines, -sines).reshape(
        row_count, kv_width
    )
    grad_proj_low = jnp.concatenate([grad_q_raw, grad_k_raw, grad_values], 1).astype(jnp.bfloat16)
    grad_one = contract_cols(grad_proj_low, back_in)
    grad_in_norm, grad_gain_one = norm_back(grad_one, inv_one, normed_one, back_gain_one)
    input_grad = grad_middle + grad_in_norm
    term_in = contract_rows(scaled_one, grad_proj_low)
    term_out = contract_rows(attended_low, grad_branch_low)
    grad_attn_in, grad_attn_out, grad_attn_gain, grad_mlp_gain = side_by_side(
        (term_in, term_out, grad_gain_one, grad_gain_two), ("dp", "ctx"), 0, 1
    )
    return (
        outputs.astype(jnp.bfloat16),
        input_grad,
        grad_attn_in,
        grad_attn_out,
        grad_attn_gain,
        grad_mlp_in,
        grad_mlp_down,
        grad_mlp_gain,
    )


def solution(mesh):
    in_specs = (
        P(("dp", "ctx"), None),
        P(("dp", "ctx")),
        P(("dp", "ctx"), None),
        P(("dp", "ctx"), None),
        P(("dp", "ctx")),
        P(("dp", "ctx"), None),
        P(("dp", "ctx"), None),
        P(("dp", "ctx")),
        P(("dp", "ctx"), None),
    )
    out_specs = (
        P(("dp", "ctx"), None),
        P(("dp", "ctx"), None),
        P(("dp", "ctx"), None),
        P(("dp", "ctx"), None),
        P(("dp", "ctx")),
        P(("dp", "ctx"), None),
        P(("dp", "ctx"), None),
        P(("dp", "ctx")),
    )
    return jax.shard_map(shards, mesh=mesh, in_specs=in_specs, out_specs=out_specs, check_vma=False)
```

profile of v0, /device:TPU:0, one launch (start us, length us, event | category | flops | bytes accessed | tf_op | source)
XLA Modules:
  0.0 1641.4 jit_solution(6918368563392712698)
XLA Ops:
  13.1 331.1 %all-gather.6.cloned.1.call-done = bf16[2048,4610]{1,0:T(8,128)(2,1)} async-done(((bf16[16,4610]{1,0:T(8,128)(2,1)}), bf16[2048,4610]{1,0:T(8,128)(2,1)}) %all-gather.6.cloned.1.call-update) | async-done | bytes 18882576 | tf_op jit(solution)/shard_map/all_gather | solution.py:24
  360.2 7.7 reshape.318
  367.9 18.0 %all_to_all.32 = bf16[8,2,16896]{2,1,0:T(2,128)(2,1)S(1)} all-to-all(bf16[8,2,16896]{2,1,0:T(2,128)(2,1)S(1)} %reshape.318), channel_id=1, replica_groups=mesh['dp'=16,'ctx'=8] {'ctx'}, dimensions={0} | all-to-all | bytes 1081344 | tf_op jit(solution)/shard_map/all_to_all | solution.py:32
  385.9 6.8 reshape.319
  403.7 7.4 fusion.90
  411.1 8.3 fusion.3
  419.4 7.6 fusion.58
  433.8 43.8 %all-gather.12.cloned.1.call-done = bf16[2048,3,704]{0,2,1:T(8,128)(2,1)} async-done(((bf16[128,3,704]{0,2,1:T(8,128)(2,1)}), bf16[2048,3,704]{0,2,1:T(8,128)(2,1)}) %all-gather.12.cloned.1.call-update) | async-done | bytes 8650768 | tf_op jit(solution)/shard_map/all_gather | solution.py:48
  477.6 52.1 %all-gather.10.cloned.1.call-done = bf16[1024,2048]{1,0:T(8,128)(2,1)} async-done(((bf16[128,2048]{1,0:T(8,128)(2,1)}), bf16[1024,2048]{1,0:T(8,128)(2,1)}) %all-gather.10.cloned.1.call-update) | async-done | bytes 4194320 | tf_op jit(solution)/shard_map/all_gather | solution.py:185
  529.7 11.0 fusion.19
  540.8 41.9 %all-gather.14.cloned.1.call-done = bf16[1024,2048]{1,0:T(8,128)(2,1)} async-done(((bf16[128,2048]{1,0:T(8,128)(2,1)}), bf16[1024,2048]{1,0:T(8,128)(2,1)}) %all-gather.14.cloned.1.call-update) | async-done | bytes 4194320 | tf_op jit(solution)/shard_map/all_gather | solution.py:201
  582.6 8.9 fusion.49
  593.1 8.3 bitcast_convert_fusion
  601.5 9.0 convolution_convert_fusion.1
  610.8 42.7 %reduce-scatter.12.cloned.1.call-done = bf16[128,2048]{1,0:T(8,128)(2,1)} async-done(((bf16[1024,2048]{1,0:T(8,128)(2,1)}), bf16[128,2048]{1,0:T(8,128)(2,1)}) %reduce-scatter.12.cloned.1.call-update) | async-done | bytes 524304 | tf_op jit(solution)/shard_map/reduce_scatter | solution.py:206
  654.9 52.9 %reduce-scatter.10.cloned.1.call-done = bf16[128,2048]{1,0:T(8,128)(2,1)} async-done(((bf16[1024,2048]{1,0:T(8,128)(2,1)}), bf16[128,2048]{1,0:T(8,128)(2,1)}) %reduce-scatter.10.cloned.1.call-update) | async-done | bytes 524304 | tf_op jit(solution)/shard_map/reduce_scatter | solution.py:194
  710.2 6.3 fusion.39
  716.8 9.4 fusion.54
  726.2 13.6 fusion
  739.9 10.2 fusion.2
  750.1 6.1 fusion.57
  758.1 8.8 fusion.25
  766.9 8.2 convolution_convert_fusion
  775.1 7.7 pad_maximum_fusion
  782.8 11.7 copy.141
  800.8 8.8 fusion.74
  810.8 9.6 fusion.70
  821.8 9.2 fusion.73
  831.0 41.8 %concatenate.59 = f32[2048,4610]{1,0:T(8,128)} concatenate(f32[2048,2560]{1,0:T(8,128)} %fusion.73, f32[2048,2048]{1,0:T(8,128)} %fusion.74, f32[2048,1]{1,0:T(8,128)} %copy.120, f32[2048,1]{1,0:T(8,128)S(1)} %copy.121), dimensions={1} | concatenate | bytes 75530240 | tf_op jit(solution)/shard_map/concatenate | solution.py:64
  872.9 30.9 %reduce-scatter.18.cloned.1.call-done = bf16[128,2112]{1,0:T(8,128)(2,1)} async-done(((bf16[2048,2112]{1,0:T(8,128)(2,1)}), bf16[128,2112]{1,0:T(8,128)(2,1)}) %reduce-scatter.18.cloned.1.call-update) | async-done | bytes 540688
  912.3 14.6 all-to-all-done.1
  929.9 699.8 %reduce-scatter.14.cloned.1.call-done = f32[16,4610]{1,0:T(8,128)} async-done(((f32[2048,4610]{1,0:T(8,128)}), f32[16,4610]{1,0:T(8,128)}) %reduce-scatter.14.cloned.1.call-update) | async-done | bytes 295056 | tf_op jit(solution)/shard_map/reduce_scatter | solution.py:65
  (162 shorter events, 72.2 us)
Async XLA Ops:
  7.2 337.1 %all-gather.6.cloned.1.call-start = ((), (), s32[]{:S(2)}) async-start(), calls=%async_computation.7 | async-start | bytes 19550208 | tf_op jit(solution)/shard_map/all_gather | solution.py:24
  10.4 391.5 %all-gather.8.cloned.1.call-start = ((), (), s32[]{:S(2)}) async-start(), calls=%async_computation.8 | async-start | bytes 1179648 | tf_op jit(solution)/shard_map/all_gather | solution.py:48
  12.3 339.4 %copy-start.23 = (f32[128]{0:T(128)}, f32[128]{0:T(128)S(1)}, u32[]{:S(2)}) copy-start(f32[128]{0:T(128)S(1)} %add_rsqrt_fusion.1) | copy-start | bytes 1540
  13.1 338.8 %copy-start.19 = (f32[128,32]{0,1:T(8,128)}, f32[128,32]{0,1:T(8,128)S(1)}, u32[]{:S(2)}) copy-start(f32[128,32]{0,1:T(8,128)S(1)} %get-tuple-element.33) | copy-start | bytes 49156
  13.1 387.8 %copy-start.14 = (f32[128,32]{0,1:T(8,128)}, f32[128,32]{0,1:T(8,128)S(1)}, u32[]{:S(2)}) copy-start(f32[128,32]{0,1:T(8,128)S(1)} %get-tuple-element.34) | copy-start | bytes 49156
  352.8 124.8 %all-gather.12.cloned.1.call-start = ((), (), s32[]{:S(2)}) async-start(), calls=%async_computation.10 | async-start | bytes 9191424 | tf_op jit(solution)/shard_map/all_gather | solution.py:48
  385.9 14.4 copy-start.25
  399.8 130.0 %all-gather.10.cloned.1.call-start = ((), (), s32[]{:S(2)}) async-start(), calls=%async_computation.9 | async-start | bytes 4718592 | tf_op jit(solution)/shard_map/all_gather | solution.py:185
  401.8 9.3 copy-start.5
  401.8 9.3 copy-start.7
  403.7 15.7 copy-start.3
  433.0 149.7 %all-gather.14.cloned.1.call-start = ((), (), s32[]{:S(2)}) async-start(), calls=%async_computation.12 | async-start | bytes 4718592 | tf_op jit(solution)/shard_map/all_gather | solution.py:201
  433.5 219.9 %reduce-scatter.12.cloned.1.call-start = ((), (), s32[]{:S(2)}) async-start(), calls=%async_computation.13 | async-start | bytes 4718592 | tf_op jit(solution)/shard_map/reduce_scatter | solution.py:206
  582.6 10.5 copy-start.26
  601.5 106.3 %reduce-scatter.10.cloned.1.call-start = ((), (), s32[]{:S(2)}) async-start(), calls=%async_computation.11 | async-start | bytes 4718592 | tf_op jit(solution)/shard_map/reduce_scatter | solution.py:194
  610.5 97.3 %copy-start.9 = (bf16[128,2048]{1,0:T(8,128)(2,1)S(1)}, bf16[128,2048]{1,0:T(8,128)(2,1)}, u32[]{:S(2)}) copy-start(bf16[128,2048]{1,0:T(8,128)(2,1)} %param.17) | copy-start | bytes 1572868
  610.5 199.1 %reduce-scatter.16.cloned.1.call-start = ((), (), s32[]{:S(2)}) async-start(), calls=%async_computation.15 | async-start | bytes 1179648
  716.8 9.5 copy-start.4
  716.8 23.0 %slice-start = ((s8[16777216]{0:T(1024)(128)(4,1)}), s8[4194304]{0:T(1024)(128)(4,1)S(1)}, s32[]{:S(2)}) async-start(s8[16777216]{0:T(1024)(128)(4,1)} %bitcast.168), calls=%async_computation.17 | async-start | bytes 8388608
  716.8 23.0 %slice-start.1 = ((s8[16777216]{0:T(1024)(128)(4,1)}), s8[4194304]{0:T(1024)(128)(4,1)S(1)}, s32[]{:S(2)}) async-start(s8[16777216]{0:T(1024)(128)(4,1)} %bitcast.168), calls=%async_computation.18 | async-start | bytes 8388608
  726.2 13.6 slice-start.2
  726.2 13.6 slice-start.3
  739.8 10.2 copy-start.6
  739.8 10.2 copy-start.8
  757.6 146.2 %reduce-scatter.18.cloned.1.call-start = ((), (), s32[]{:S(2)}) async-start(), calls=%async_computation.16 | async-start | bytes 9469952
  758.0 8.8 copy-start.27
  758.0 8.8 copy-start.29
  794.5 835.3 %reduce-scatter.14.cloned.1.call-start = ((), (), s32[]{:S(2)}) async-start(), calls=%async_computation.14 | async-start | bytes 39100416 | tf_op jit(solution)/shard_map/reduce_scatter | solution.py:65
  800.7 10.1 copy-start.22
  800.8 10.1 copy-start.24
  872.8 38.1 %copy-start.11 = (f32[128,2048]{1,0:T(8,128)S(1)}, f32[128,2048]{1,0:T(8,128)}, u32[]{:S(2)}) copy-start(f32[128,2048]{1,0:T(8,128)} %get-tuple-element.41) | copy-start | bytes 3145732
  906.6 20.3 %all-to-all-start.1 = ((bf16[128,3,704]{2,1,0:T(4,128)(2,1)}), bf16[128,3,704]{2,1,0:T(4,128)(2,1)S(1)}, u32[]{:S(2)}, u32[]{:S(2)}) async-start(bf16[128,3,704]{2,1,0:T(4,128)(2,1)} %copy.122), calls=%async_computation.4 | async-start | bytes 1572864 | tf_op jit(solution)/shard_map/all_to_all | solution.py:224
  (15 other events, 80.1 us)
Sparse Core Ops, SparseCore 0:
  10.5 333.6 all-gather.5
  352.9 40.5 all-gather.7
  399.9 77.6 all-gather.11
  479.7 50.0 all-gather.9
  531.2 51.3 all-gather.13
  601.6 51.8 reduce-scatter.11
  655.9 51.8 reduce-scatter.9
  757.7 37.8 reduce-scatter.15
  800.0 103.7 reduce-scatter.17
  906.2 723.5 reduce-scatter.13
where the time goes:
time: 1650 us; the launch traced here: 1640 us
  waiting for transfers between devices  1310 us (79%)
  matrix products  147 us (9%)
  local copies, waits for them, and re-layouts  104 us (6%)
  other arithmetic  40.3 us (2%)
  blocking collectives  18 us (1%)
    reduce_scatter x1, waiting for transfers between devices, side_by_side(): lax.psum_scatter(both, axis, scatter_dimension=dim, tiled=True)  700 us
    all_gather x1, waiting for transfers between devices, in_one_piece(): out = lax.all_gather(both, axis, axis=dim, tiled=True)  331 us
    reduce_scatter x1, waiting for transfers between devices, shards(): lax.psum_scatter(contract_cols(hidden_act, down_block).astype(jnp.bfloat1...  52.9 us
    all_gather x1, waiting for transfers between devices, shards(): seq_scaled = lax.all_gather(scaled_two, 'ctx', axis=0, tiled=True)  52.1 us
    all_gather x2, waiting for transfers between devices, in_one_piece_3(): lax.all_gather(both, axis, axis=dim, tiled=True)  43.9 us
    reduce_scatter x1, waiting for transfers between devices, shards(): lax.psum_scatter(jnp.einsum('tkf,dkf->td', grad_gu_low, back_gu, preferre...  42.7 us
    all_gather x1, waiting for transfers between devices, shards(): seq_grad = lax.all_gather(cotangent, 'ctx', axis=0, tiled=True)  41.9 us
    concatenate x1, local copies, waits for them, and re-layouts, side_by_side(): both = jnp.concatenate(columns, axis=along)  41.8 us
  transfers between devices with their start and end apart: 11, of which 9 were waited for; matrix products, arithmetic and copies ran while one was open for 13% of the time, Pallas kernels for 0%

commit v1 on v0

v1 whole, which is shorter than its diff:
```python
import jax
import jax.numpy as jnp
from jax import lax
from jax.experimental import pallas as pl
from jax.experimental.pallas import tpu as pltpu
from jax.sharding import PartitionSpec as P


D = 2048
HEADS = 32
KV_HEADS = 4
HEAD_DIM = 64
FF = 5632
REPEAT = HEADS // KV_HEADS
TP = 4
Q_COLS = D // TP
PROJ = Q_COLS + 2 * HEAD_DIM
HID = FF // TP

EPS = 1e-05
ROPE_BASE = 10000.0
NEG_FILL = -1e30

MESH = pl.DeviceIdType.MESH
BF16 = jnp.bfloat16
F32 = jnp.float32

SPLITS = ((PROJ, 384), (2 * HID, HID), (HID, 640))
OUT_SPLIT = 1024


def place():
    dp, ctx = lax.axis_index("dp"), lax.axis_index("ctx")
    return (dp // 2) % 2, ctx // 4, ctx % 4, dp // 4, dp % 2


def device(xh, xl, y, z, c):
    return (z * 4 + xh * 2 + c, xl * 4 + y)


def along_y(d):
    def to(xh, xl, y, z, c):
        return xh, xl, (y + d) % 4, z, c

    return to


def along_x(d):
    def to(xh, xl, y, z, c):
        x = (xh * 2 + xl + d) % 4
        return x // 2, x % 2, y, z, c

    return to


def along_z(d):
    def to(xh, xl, y, z, c):
        return xh, xl, y, (z + d) % 4, c

    return to


def sibling(xh, xl, y, z, c):
    return xh, xl, y, z, 1 - c


def half_partner(xh, xl, y, z, c):
    return xh, 1 - xl, y, z, c


def crossed(xh, xl, y, z, c):
    return xh, xl, z, y, c


def greet(routes, cross):
    here = place()
    barrier = pltpu.get_barrier_semaphore()
    for back in routes:
        pl.semaphore_signal(barrier, inc=1, device_id=device(*back(*here)), device_id_type=MESH)
    if not cross:
        pl.semaphore_wait(barrier, len(routes))
        return
    away = here[2] != here[3]

    @pl.when(away)
    def _():
        pl.semaphore_signal(barrier, inc=1, device_id=device(*crossed(*here)), device_id_type=MESH)
        pl.semaphore_wait(barrier, len(routes) + 1)

    @pl.when(jnp.logical_not(away))
    def _():
        pl.semaphore_wait(barrier, len(routes))


class Copies:
    def __init__(self, send, recv):
        self.send, self.recv, self.count = send, recv, 0

    def __call__(self, src, dst, to):
        k, self.count = self.count, self.count + 1
        return pltpu.make_async_remote_copy(
            src_ref=src,
            dst_ref=dst,
            send_sem=self.send.at[k],
            recv_sem=self.recv.at[k],
            device_id=device(*to(*place())),
            device_id_type=MESH,
        )


def comm_call(kernel, name, ident, ins, outs, copies, locals_=0):
    return pl.pallas_call(
        kernel,
        out_shape=outs,
        in_specs=[pl.BlockSpec(memory_space=pl.ANY)] * len(ins),
        out_specs=[pl.BlockSpec(memory_space=pl.ANY)] * len(outs),
        scratch_shapes=[
            pltpu.SemaphoreType.DMA((copies,)),
            pltpu.SemaphoreType.DMA((copies,)),
            pltpu.SemaphoreType.DMA((max(locals_, 1),)),
        ],
        name=name,
        compiler_params=pltpu.CompilerParams(collective_id=ident, has_side_effects=True),
    )(*ins)


def struct(shape, dtype=BF16):
    return jax.ShapeDtypeStruct(shape, dtype)


def ring_gather(parts, ident, name):
    n = len(parts)

    def kernel(*refs):
        ins, outs, (send, recv, local) = refs[:n], refs[n : 2 * n], refs[2 * n :]
        xh, xl, y, z, c = place()
        greet([along_y(d) for d in (1, 2, 3)], False)
        copy = Copies(send, recv)
        going = []
        for i, o in zip(ins, outs):
            for d in (1, 3, 2):
                going.append(copy(i, o.at[y], along_y(d)))
                going[-1].start()
        own = [pltpu.make_async_copy(i, o.at[y], local.at[k]) for k, (i, o) in enumerate(zip(ins, outs))]
        for cp in own:
            cp.start()
        for cp in going:
            cp.wait()
        for cp in own:
            cp.wait()

    return comm_call(
        kernel, name, ident, parts, [struct((4,) + p.shape, p.dtype) for p in parts], 3 * n, n
    )


def ring_scatter(part, ident, name):
    def kernel(src, dst, send, recv, local):
        xh, xl, y, z, c = place()
        greet([along_y(d) for d in (1, 2, 3)], False)
        copy = Copies(send, recv)
        going = []
        for d in (1, 3, 2):
            going.append(copy(src.at[(y + d) % 4], dst.at[d - 1], along_y(d)))
            going[-1].start()
        for cp in going:
            cp.wait()

    (out,) = comm_call(kernel, name, ident, [part], [struct((3,) + part.shape[1:])], 3)
    return out


def ring_sum(part, ident, name):
    part = part.reshape(4, part.shape[0] // 4, part.shape[1])
    own = lax.dynamic_index_in_dim(part, lax.axis_index("ctx") % 4, 0, keepdims=False)
    others = ring_scatter(part, ident, name)
    return own.astype(F32) + jnp.sum(others.astype(F32), 0)


def swap(part, to, ident, name):
    def kernel(src, dst, send, recv, local):
        greet([to], False)
        cp = Copies(send, recv)(src, dst, to)
        cp.start()
        cp.wait()

    (out,) = comm_call(kernel, name, ident, [part], [struct(part.shape, part.dtype)], 1)
    return out


def gather_weights(blocks, out_rows, ident):
    n = len(blocks)

    def kernel(*refs):
        ins, rows_in = refs[:n], refs[n]
        outs, rows_out = refs[n + 1 : 2 * n + 1], refs[2 * n + 1]
        send, recv, local = refs[2 * n + 2 :]
        xh, xl, y, z, c = place()
        greet(
            [along_y(d) for d in (1, 2, 3)]
            + [along_x(d) for d in (1, 2, 3)]
            + [along_z(d) for d in (1, 2, 3)]
            + [sibling],
            True,
        )
        copy = Copies(send, recv)
        mine = pl.ds(xl * 64, 64)
        slot = pl.ds(xl * 64 + y * 16, 16)
        started = []

        def go(src, dst, to):
            cp = copy(src, dst, to)
            cp.start()
            started.append(cp)
            return cp

        first = []
        for i, o in zip(ins, outs):
            for d in (1, 3, 2):
                first.append(go(i.at[(y + d) % 4], o.at[z, xh, c, slot], along_y(d)))
        over = copy(rows_in, rows_out.at[xh, c, xl, y], crossed)
        away = y != z

        @pl.when(away)
        def _():
            over.start()

        own = [
            pltpu.make_async_copy(i.at[y], o.at[z, xh, c, slot], local.at[k])
            for k, (i, o) in enumerate(zip(ins, outs))
        ]
        for cp in own:
            cp.start()
        stay = pltpu.make_async_copy(rows_in, rows_out.at[xh, c, xl, z], local.at[n])

        @pl.when(jnp.logical_not(away))
        def _():
            stay.start()
            stay.wait()

        for cp in own:
            cp.wait()
        for cp in first:
            cp.wait_recv()

        @pl.when(away)
        def _():
            over.wait()

        a_first, b_first = [], []
        for o, (cols, a) in zip(outs, SPLITS):
            left, right = pl.ds(0, a), pl.ds(a, cols - a)
            for d in (1, 3, 2):
                a_first.append(go(o.at[z, xh, c, mine, left], o.at[z, xh, c, mine, left], along_x(d)))
                b_first.append(go(o.at[z, xh, c, mine, right], o.at[z, xh, c, mine, right], along_z(d)))
        left, right = pl.ds(0, OUT_SPLIT), pl.ds(OUT_SPLIT, D - OUT_SPLIT)
        for d in (1, 3, 2):
            at = rows_out.at[xh, c, xl, z, :, left]
            a_first.append(go(at, at, along_x(d)))
            at = rows_out.at[xh, c, xl, z, :, right]
            b_first.append(go(at, at, along_z(d)))
        cores = []
        for o in outs:
            cores.append(go(o.at[z, xh, c, mine], o.at[z, xh, c, mine], sibling))
        at = rows_out.at[xh, c, xl, z]
        cores.append(go(at, at, sibling))
        for cp in a_first + b_first:
            cp.wait_recv()

        a_second, b_second = [], []
        for d in (1, 3, 2):
            for o, (cols, a) in zip(outs, SPLITS):
                left, right = pl.ds(0, a), pl.ds(a, cols - a)
                at = o.at[z, :, c, :, left]
                a_second.append(go(at, at, along_z(d)))
                at = o.at[:, xh, c, mine, right]
                b_second.append(go(at, at, along_x(d)))
            left, right = pl.ds(0, OUT_SPLIT), pl.ds(OUT_SPLIT, D - OUT_SPLIT)
            at = rows_out.at[:, c, :, z, :, left]
            a_second.append(go(at, at, along_z(d)))
            at = rows_out.at[xh, c, xl, :, :, right]
            b_second.append(go(at, at, along_x(d)))

        for d in (1, 3, 2):
            fx, fxl, _, _, _ = along_x(4 - d)(xh, xl, y, z, c)
            fz = (z + 4 - d) % 4
            theirs = pl.ds(fxl * 64, 64)
            for o, (cols, a) in zip(outs, SPLITS):
                left, right = pl.ds(0, a), pl.ds(a, cols - a)
                at = o.at[z, fx, c, theirs, left]
                cores.append(go(at, at, sibling))
                at = o.at[fz, xh, c, mine, right]
                cores.append(go(at, at, sibling))
            left, right = pl.ds(0, OUT_SPLIT), pl.ds(OUT_SPLIT, D - OUT_SPLIT)
            at = rows_out.at[fx, c, fxl, z, :, left]
            cores.append(go(at, at, sibling))
            at = rows_out.at[xh, c, xl, fz, :, right]
            cores.append(go(at, at, sibling))

        at_a, at_b = iter(a_second), iter(b_second)
        for d in (1, 3, 2):
            fx, fxl, _, _, _ = along_x(4 - d)(xh, xl, y, z, c)
            fz = (z + 4 - d) % 4
            theirs = pl.ds(fxl * 64, 64)
            for o, (cols, a) in zip(outs, SPLITS):
                left, right = pl.ds(0, a), pl.ds(a, cols - a)
                next(at_a).wait_recv()
                at = o.at[fz, :, c, :, left]
                cores.append(go(at, at, sibling))
                next(at_b).wait_recv()
                at = o.at[:, fx, c, theirs, right]
                cores.append(go(at, at, sibling))
            left, right = pl.ds(0, OUT_SPLIT), pl.ds(OUT_SPLIT, D - OUT_SPLIT)
            next(at_a).wait_recv()
            at = rows_out.at[:, c, :, fz, :, left]
            cores.append(go(at, at, sibling))
            next(at_b).wait_recv()
            at = rows_out.at[fx, c, fxl, :, :, right]
            cores.append(go(at, at, sibling))
        for cp in cores:
            cp.wait_recv()
        for cp in started:
            cp.wait_send()

    outs = [struct((4, 2, 2, 128, b.shape[2])) for b in blocks] + [struct((2, 2, 2, 4, 16, D))]
    copies = 3 * n + 1 + 7 * 3 * (n + 1) * 2
    got = comm_call(kernel, "gather_weights", ident, [*blocks, out_rows], outs, copies, n + 1)
    return [g.reshape(D, g.shape[-1]) for g in got[:-1]] + [got[-1].reshape(Q_COLS, D)]


def across(parts, rows_part, ident, name, stage):
    n = len(SPLITS)
    everything = [*parts, rows_part]
    if stage == "core":
        routes = [sibling]
    elif stage == "y":
        routes = [along_y(d) for d in (1, 2, 3)]
    else:
        routes = [along_x(d) for d in (1, 2, 3)] + [along_z(d) for d in (1, 2, 3)]

    if stage == "core":
        outs = [struct(p.shape[:2] + p.shape[3:]) for p in parts] + [struct((2, 2, 4, 16, D))]
    elif stage == "first":
        outs = []
        for cols, a in SPLITS:
            outs += [struct((3, 2, 128, a)), struct((3, 4, 64, cols - a))]
        outs += [struct((3, 2, 2, 16, OUT_SPLIT)), struct((3, 4, 16, D - OUT_SPLIT))]
    elif stage == "second":
        outs = []
        for cols, a in SPLITS:
            outs += [struct((3, 64, a)), struct((3, 64, cols - a))]
        outs += [struct((3, 16, OUT_SPLIT)), struct((3, 16, D - OUT_SPLIT))]
    else:
        outs = [struct(p.shape) for p in parts] + [struct(rows_part.shape)]

    def kernel(*refs):
        ins, dsts = refs[: len(everything)], refs[len(everything) : len(everything) + len(outs)]
        send, recv, local = refs[len(everything) + len(outs) :]
        xh, xl, y, z, c = place()
        greet(routes, stage == "y")
        copy = Copies(send, recv)
        going = []
        if stage == "core":
            for i, o in zip(ins[:n], dsts[:n]):
                going.append(copy(i.at[:, :, 1 - c], o, sibling))
            going.append(copy(ins[n].at[:, 1 - c], dsts[n], sibling))
        elif stage == "first":
            for d in (1, 3, 2):
                tx, txl, _, _, _ = along_x(d)(xh, xl, y, z, c)
                tz = (z + d) % 4
                theirs = pl.ds(txl * 64, 64)
                for k, (cols, a) in enumerate(SPLITS):
                    left, right = pl.ds(0, a), pl.ds(a, cols - a)
                    going.append(copy(ins[k].at[tz, :, :, left], dsts[2 * k].at[d - 1], along_z(d)))
                    going.append(
                        copy(ins[k].at[:, tx, theirs, right], dsts[2 * k + 1].at[d - 1], along_x(d))
                    )
                left, right = pl.ds(0, OUT_SPLIT), pl.ds(OUT_SPLIT, D - OUT_SPLIT)
                going.append(copy(ins[n].at[:, :, tz, :, left], dsts[2 * n].at[d - 1], along_z(d)))
                going.append(
                    copy(ins[n].at[tx, txl, :, :, right], dsts[2 * n + 1].at[d - 1], along_x(d))
                )
        elif stage == "second":
            for d in (1, 3, 2):
                tx, txl, _, _, _ = along_x(d)(xh, xl, y, z, c)
                tz = (z + d) % 4
                theirs = pl.ds(txl * 64, 64)
                for k in range(n):
                    going.append(copy(ins[2 * k].at[tx, theirs], dsts[2 * k].at[d - 1], along_x(d)))
                    going.append(copy(ins[2 * k + 1].at[tz], dsts[2 * k + 1].at[d - 1], along_z(d)))
                going.append(copy(ins[2 * n].at[tx, txl], dsts[2 * n].at[d - 1], along_x(d)))
                going.append(copy(ins[2 * n + 1].at[tz], dsts[2 * n + 1].at[d - 1], along_z(d)))
        else:
            for i, o in zip(ins[:n], dsts[:n]):
                for d in (1, 3, 2):
                    going.append(copy(i.at[(y + d) % 4], o.at[y], along_y(d)))
            over = copy(ins[n], dsts[n], crossed)
        for cp in going:
            cp.start()
        if stage == "y":
            away = y != z
            stay = pltpu.make_async_copy(ins[n], dsts[n], local.at[n])

            @pl.when(away)
            def _():
                over.start()

            @pl.when(jnp.logical_not(away))
            def _():
                stay.start()
                stay.wait()

            own = [
                pltpu.make_async_copy(i.at[y], o.at[y], local.at[k])
                for k, (i, o) in enumerate(zip(ins[:n], dsts[:n]))
            ]
            for cp in own:
                cp.start()
            for cp in own:
                cp.wait()

            @pl.when(away)
            def _():
                over.wait()

        for cp in going:
            cp.wait()

    return comm_call(kernel, name, ident, everything, outs, 6 * (n + 1) + 1, n + 1)


def total(own, others):
    return (own.astype(F32) + jnp.sum(others.astype(F32), 0)).astype(BF16)


def scatter_grads(blocks, rows_block, idents):
    xh, xl, y, z, c = place()
    n = len(blocks)
    pick = lax.dynamic_index_in_dim
    parts = [b.reshape(4, 2, 2, 128, b.shape[1]) for b in blocks]
    rows_part = rows_block.reshape(2, 2, 2, 4, 16, D)
    got = across(parts, rows_part, idents[0], "grads_core", "core")
    parts = [total(pick(p, c, 2, False), g[None]) for p, g in zip(parts, got)]
    rows_part = total(pick(rows_part, c, 1, False), got[n][None])
    got = across(parts, rows_part, idents[1], "grads_first", "first")
    second = []
    for k, (cols, a) in enumerate(SPLITS):
        mine = pick(parts[k], z, 0, False)[..., :a]
        second.append(total(mine, got[2 * k]))
        mine = lax.dynamic_slice_in_dim(pick(parts[k], xh, 1, False), xl * 64, 64, 1)[..., a:]
        second.append(total(mine, got[2 * k + 1]))
    second.append(total(pick(rows_part, z, 2, False)[..., :OUT_SPLIT], got[2 * n]))
    second_rows = total(pick(pick(rows_part, xh, 0, False), xl, 0, False)[..., OUT_SPLIT:], got[2 * n + 1])
    got = across(second, second_rows, idents[2], "grads_second", "second")
    last = []
    for k in range(n):
        left = lax.dynamic_slice_in_dim(pick(second[2 * k], xh, 0, False), xl * 64, 64, 0)
        left = total(left, got[2 * k])
        right = total(pick(second[2 * k + 1], z, 0, False), got[2 * k + 1])
        last.append(jnp.concatenate([left, right], -1).reshape(4, 16, -1))
    left = total(pick(pick(second[2 * n], xh, 0, False), xl, 0, False), got[2 * n])
    right = total(pick(second_rows, z, 0, False), got[2 * n + 1])
    return across(last, jnp.concatenate([left, right], -1), idents[3], "grads_y", "y")


def angles(positions):
    inv_freq = ROPE_BASE ** (-jnp.arange(0, HEAD_DIM, 2, dtype=F32) / HEAD_DIM)
    phase = positions.astype(F32)[:, None] * inv_freq[None, :]
    return jnp.cos(phase)[:, None, :], jnp.sin(phase)[:, None, :]


def rotary(values, cosines, sines):
    half = values.shape[-1] // 2
    first, second = values[..., :half], values[..., half:]
    return jnp.concatenate([first * cosines - second * sines, second * cosines + first * sines], -1)


def inv_norm(values):
    return lax.rsqrt(jnp.mean(values * values, -1, keepdims=True) + EPS)


def norm_back(grad_normed, inv_root, normed):
    return inv_root * (grad_normed - normed * jnp.mean(grad_normed * normed, -1, keepdims=True))


def mm(left, right, dims, out=F32):
    return lax.dot_general(left, right, (dims, ((), ())), preferred_element_type=F32).astype(out)


NN = ((1,), (0,))
NT = ((1,), (1,))
TN = ((0,), (0,))


def shards(tokens, positions, attn_in, attn_out, attn_gain, mlp_in, mlp_down, mlp_gain, cotangent):
    xh, xl, y, z, c = place()
    rows = tokens.shape[0]
    count = 4 * rows
    scale = HEAD_DIM ** (-0.5)
    gain_one = attn_gain.astype(F32)[:, None]
    gain_two = mlp_gain.astype(F32)[:, None]

    in_f = attn_in.astype(F32)
    mlp_f = mlp_in.astype(F32)
    kv = HEAD_DIM * KV_HEADS
    by_y = lambda a: a.reshape(16, TP, -1)
    w_proj = jnp.concatenate(
        [by_y(in_f[:, :D]), by_y(in_f[:, D : D + kv]), by_y(in_f[:, D + kv :])], -1
    )
    w_proj = (w_proj * gain_one[:, :, None]).astype(BF16).transpose(1, 0, 2)
    w_gu = jnp.concatenate([by_y(mlp_f[:, :FF]), by_y(mlp_f[:, FF:])], -1)
    w_gu = (w_gu * gain_two[:, :, None]).astype(BF16).transpose(1, 0, 2)
    w_down = by_y(mlp_down).transpose(1, 0, 2)
    proj_w, gu_w, down_w, out_w = gather_weights([w_proj, w_gu, w_down], attn_out, 0)

    spots = jnp.broadcast_to(positions[None, :], (8, rows))
    tokens_all, cot_all, spots_all = ring_gather([tokens, cotangent, spots], 1, "gather_tokens")
    seq_tokens = tokens_all.reshape(count, D).astype(F32)
    seq_cot = cot_all.reshape(count, D)
    seq_pos = spots_all[:, 0].reshape(count)

    normed_one_all = (seq_tokens * inv_norm(seq_tokens)).astype(BF16)
    projected = mm(normed_one_all, proj_w, NN)
    cosines, sines = angles(seq_pos)
    queries = rotary(projected[:, :Q_COLS].reshape(count, REPEAT, HEAD_DIM), cosines, sines).astype(BF16)
    keys = rotary(projected[:, None, Q_COLS : Q_COLS + HEAD_DIM], cosines, sines)[:, 0].astype(BF16)
    keys_values = jnp.concatenate([keys, projected[:, Q_COLS + HEAD_DIM :].astype(BF16)], -1)
    theirs = swap(keys_values, half_partner, 2, "swap_keys")
    low_half = xl == 0
    kv_all = jnp.concatenate(
        [jnp.where(low_half, keys_values, theirs), jnp.where(low_half, theirs, keys_values)], 0
    )
    keys_all, values_all = kv_all[:, :HEAD_DIM], kv_all[:, HEAD_DIM:]
    query_index = xl * count + jnp.arange(count, dtype=jnp.int32)
    key_index = jnp.arange(2 * count, dtype=jnp.int32)
    visible = (key_index[None, :] <= query_index[:, None]) & (
        query_index[:, None] - key_index[None, :] <= seq_pos[:, None]
    )

    def masked_scores():
        raw = jnp.einsum("qhd,kd->hqk", queries, keys_all, preferred_element_type=F32)
        return jnp.where(visible[None], raw * scale, NEG_FILL)

    scores = masked_scores()
    peak = jnp.max(scores, -1, keepdims=True)
    exps = jnp.exp(scores - peak)
    row_total = jnp.sum(exps, -1, keepdims=True)
    probs_low = (exps / row_total).astype(BF16)
    log_total = peak + jnp.log(row_total)
    attended = jnp.einsum("hqk,kd->qhd", probs_low, values_all, preferred_element_type=F32)
    attended_low = attended.reshape(count, Q_COLS).astype(BF16)
    branch = ring_sum(mm(attended_low, out_w, NN, BF16), 3, "sum_branch")
    inputs = tokens.astype(F32)
    middle = inputs + branch
    inv_two = inv_norm(middle)
    normed_two = middle * inv_two
    (seq_two,) = ring_gather([normed_two.astype(BF16)], 4, "gather_two")
    seq_two = seq_two.reshape(count, D)

    gate_up = mm(seq_two, gu_w, NN)
    gate, up = gate_up[:, :HID], gate_up[:, HID:]
    gate_sigmoid = jax.nn.sigmoid(gate)
    gate_silu = gate * gate_sigmoid
    hidden_act = (gate_silu * up).astype(BF16)
    outputs = middle + ring_sum(mm(hidden_act, down_w, NT, BF16), 5, "sum_outputs")

    grad_hidden = mm(seq_cot, down_w, NN)
    grad_gate = grad_hidden * up * gate_sigmoid * (1.0 + gate * (1.0 - gate_sigmoid))
    grad_gu = jnp.concatenate([grad_gate, grad_hidden * gate_silu], -1).astype(BF16)
    grad_two = ring_sum(mm(grad_gu, gu_w, NT, BF16), 6, "sum_grad_two")
    grad_middle = cotangent.astype(F32) + norm_back(grad_two, inv_two, normed_two)
    term_gu = mm(seq_two, grad_gu, TN, BF16)
    term_down = mm(seq_cot, hidden_act, TN, BF16)

    (seq_branch,) = ring_gather([grad_middle.astype(BF16)], 7, "gather_branch")
    seq_branch = seq_branch.reshape(count, D)
    grad_att = mm(seq_branch, out_w, NT, BF16).reshape(count, REPEAT, HEAD_DIM)
    probs = jnp.exp(masked_scores() - log_total)
    grad_probs = jnp.einsum("qhd,kd->hqk", grad_att, values_all, preferred_element_type=F32)
    row_delta = jnp.sum(probs * grad_probs, -1, keepdims=True)
    grad_scores = (probs * (grad_probs - row_delta)).astype(BF16)
    grad_q = jnp.einsum("hqk,kd->qhd", grad_scores, keys_all, preferred_element_type=F32) * scale
    grad_k = jnp.einsum("hqk,qhd->kd", grad_scores, queries, preferred_element_type=F32) * scale
    grad_v = jnp.einsum("hqk,qhd->kd", probs.astype(BF16), grad_att, preferred_element_type=F32)
    grad_kv = jnp.concatenate([grad_k, grad_v], -1).reshape(2, count, 2 * HEAD_DIM)
    away = lax.dynamic_index_in_dim(grad_kv, 1 - xl, 0, False).astype(BF16)
    grad_kv = lax.dynamic_index_in_dim(grad_kv, xl, 0, False)
    grad_kv = grad_kv + swap(away, half_partner, 8, "swap_grad_keys").astype(F32)
    grad_q = rotary(grad_q, cosines, -sines).reshape(count, Q_COLS)
    grad_k = rotary(grad_kv[:, None, :HEAD_DIM], cosines, -sines)[:, 0]
    grad_proj = jnp.concatenate([grad_q, grad_k, grad_kv[:, HEAD_DIM:]], -1).astype(BF16)
    grad_one = ring_sum(mm(grad_proj, proj_w, NT, BF16), 9, "sum_grad_one")
    inv_one = inv_norm(inputs)
    input_grad = grad_middle + norm_back(grad_one, inv_one, inputs * inv_one)
    term_proj = mm(normed_one_all, grad_proj, TN, BF16)
    term_out = mm(attended_low, seq_branch, TN, BF16)

    own_proj, own_gu, own_down, own_out = scatter_grads(
        [term_proj, term_gu, term_down], term_out, (10, 11, 12, 13)
    )
    own_proj = own_proj.astype(F32).transpose(1, 0, 2)
    cut = lambda a, start, stop: a[:, :, start:stop].reshape(16, -1)
    own_proj = jnp.concatenate(
        [
            cut(own_proj, 0, Q_COLS),
            cut(own_proj, Q_COLS, Q_COLS + HEAD_DIM),
            cut(own_proj, Q_COLS + HEAD_DIM, PROJ),
        ],
        -1,
    )
    own_gu = own_gu.astype(F32).transpose(1, 0, 2)
    own_gu = jnp.concatenate([cut(own_gu, 0, HID), cut(own_gu, HID, 2 * HID)], -1)
    own_down = own_down.astype(F32).transpose(1, 0, 2).reshape(16, FF)
    return (
        outputs.astype(BF16),
        input_grad,
        own_proj * gain_one,
        own_out.astype(F32),
        jnp.sum(own_proj * in_f, -1),
        own_gu * gain_two,
        own_down,
        jnp.sum(own_gu * mlp_f, -1),
    )


def solution(mesh):
    both = ("dp", "ctx")
    wide, flat = P(both, None), P(both)
    in_specs = (wide, flat, wide, wide, flat, wide, wide, flat, wide)
    out_specs = (wide, wide, wide, wide, flat, wide, wide, flat)
    return jax.shard_map(shards, mesh=mesh, in_specs=in_specs, out_specs=out_specs, check_vma=False)
```

time: 1650 us -> 659 us (0.40)
  waiting for transfers between devices: 1310 us -> 0 us
  Pallas kernels: 0 us -> 426 us
  local copies, waits for them, and re-layouts: 104 us -> 25.6 us
  other arithmetic: 40.3 us -> 91.6 us
  matrix products: 147 us -> 107 us
  blocking collectives: 18 us -> 0 us
    reduce_scatter x3 -> x0, waiting for transfers between devices: 795 us -> none  [the longest x1 700 us: side_by_side(): lax.psum_scatter(both, axis, scatter_dimension=dim, tiled=True)]
    all_gather x5 -> x0, waiting for transfers between devices: 469 us -> none  [the longest x1 331 us: in_one_piece(): out = lax.all_gather(both, axis, axis=dim, tiled=True)]
    pallas_call x0 -> x14, Pallas kernels: none -> 426 us  [comm_call(): pl.pallas_call(kernel, out_shape=outs, in_specs=[pl.BlockSpec(memory_spac...]
    concatenate x3, local copies, waits for them, and re-layouts: 49.4 us -> 0.22 us  [the longest x1 0.19 us: shards(): jnp.concatenate([grad_k, grad_v], -1).reshape(2, count, 2 * HEAD_DIM)]
    dot_general x18, matrix products: 147 us -> 107 us  [the longest x12 67.6 us: mm(): lax.dot_general(left, right, (dims, ((), ())), preferred_element_type=F32)]
    unnamed x12 -> x0, waiting for transfers between devices: 31.6 us -> none
    convert_element_type x5 -> x30, other arithmetic: 14.3 us -> 40.5 us  [the longest x20 25.1 us: total(): return (own.astype(F32) + jnp.sum(others.astype(F32), 0)).astype(BF16)]
    unnamed x80 -> x169, local copies, waits for them, and re-layouts: 31.3 us -> 7.35 us
  transfers between devices with their start and end apart: 11 -> 0, of which waited for: 9 -> 0; matrix products, arithmetic and copies ran while one was open for 13% -> 0% of each run, Pallas kernels for 0% -> 0%
where the time goes in v1:
time: 659 us; the launch traced here: 653 us
  Pallas kernels  426 us (65%)
  matrix products  107 us (16%)
  other arithmetic  91.6 us (14%)
  local copies, waits for them, and re-layouts  25.6 us (4%)
    pallas_call x14, Pallas kernels, comm_call(): pl.pallas_call(kernel, out_shape=outs, in_specs=[pl.BlockSpec(memory_spac...  426 us
    dot_general x12, matrix products, mm(): lax.dot_general(left, right, (dims, ((), ())), preferred_element_type=F32)  67.6 us
    convert_element_type x20, other arithmetic, total(): return (own.astype(F32) + jnp.sum(others.astype(F32), 0)).astype(BF16)  25.1 us

profile of v1, /device:TPU:0, one launch (start us, length us, event | category | flops | bytes accessed | tf_op | source)
XLA Modules:
  0.0 652.6 jit_solution(682406904003282771)
XLA Ops:
  1.9 50.6 %gather_tokens.1 = (bf16[4,128,2048]{2,1,0:T(8,128)(2,1)}, bf16[4,128,2048]{2,1,0:T(8,128)(2,1)}, s32[4,8,128]{2,1,0:T(8,128)}) custom-call(bf16[128,2048]{1,0:T(8,128)(2,1)} %refs_0_.1, bf16[128,2048]{1,0:T(8,128)(2,1)} %refs_1_.1, s32[8,128]{1,0:T(8,128)} %broadcast_in_dim.18.refs_2_), custom_call_target="tpu_custom_call" | custom-call | tf_op jit(solution)/shard_map/gather_tokens/pallas_call | solution.py:112
  59.8 97.2 %gather_weights.1 = (bf16[4,2,2,128,640]{4,3,2,1,0:T(8,128)(2,1)}, bf16[4,2,2,128,2816]{4,3,2,1,0:T(8,128)(2,1)}, bf16[4,2,2,128,1408]{4,3,2,1,0:T(8,128)(2,1)}, bf16[2,2,2,4,16,2048]{5,4,3,2,1,0:T(8,128)(2,1)}) custom-call(bf16[4,16,640]{2,1,0:T(8,128)(2,1)} %fusion.60.refs_0_, bf16[4,16,2816]{2,1,0:T(8,128)(2,1)} %fusion.39.refs_1_, ...), custom_call_target="tpu_custom_call" | custom-call | tf_op jit(solution)/shard_map/gather_weights/pallas_call | solution.py:112
  156.9 4.2 fusion.81
  170.9 6.3 swap_keys.1
  178.9 7.2 %fusion.80 = (f32[8,512]{1,0:T(8,128)S(1)}, f32[8,512,1024]{1,2,0:T(8,128)}) fusion(bf16[512,8,32]{0,2,1:T(8,128)(2,1)S(1)} %get-tuple-element.80, bf16[512,8,32]{0,2,1:T(8,128)(2,1)S(1)} %get-tuple-element.79, bf16[512,128]{1,0:T(8,128)(2,1)S(1)} %get-tuple-element.94, bf16[512,128]{1,0:T(8,128)(2,1)S(1)} %get-tuple-element.93, ...), kind=kOutput, calls=%fused_computation.225 | convolution fusion | flops 550760448 | bytes 18104320 | tf_op jit(solution)/shard_map/qhd,kd->hqk/dot_general | solution.py:541
  186.1 8.0 %fusion.3 = f32[8,512]{1,0:T(8,128)S(1)} fusion(f32[8,512,1024]{1,2,0:T(8,128)} %get-tuple-element.107, f32[8,512]{1,0:T(8,128)S(1)} %get-tuple-element.106), kind=kLoop, calls=%fused_computation.9 | loop fusion | flops 8384512 | bytes 16809984 | tf_op jit(solution)/shard_map/reduce_sum | solution.py:547
  194.1 7.9 %fusion.17 = bf16[64,8,512]{2,0,1:T(8,128)(2,1)S(1)} fusion(f32[8,512,1024]{1,2,0:T(8,128)} %get-tuple-element.107, f32[8,512]{1,0:T(8,128)S(1)} %fusion.3, f32[8,512]{1,0:T(8,128)S(1)} %get-tuple-element.106, bf16[512,128]{1,0:T(8,128)(2,1)S(1)} %get-tuple-element.94, bf16[512,128]{1,0:T(8,128)(2,1)S(1)} %get-tuple-element.93), kind=kOutput, calls=%fused_computation.61 | convolution fusion | flops 549978112 | bytes 17596416 | tf_op jit(solution)/shard_map/hqk,kd->qhd/dot_general | solution.py:550
  204.7 34.0 %sum_branch.1 = bf16[3,128,2048]{2,1,0:T(8,128)(2,1)} custom-call(bf16[4,128,2048]{2,1,0:T(8,128)(2,1)} %bitcast.232), custom_call_target="tpu_custom_call" | custom-call | tf_op jit(solution)/shard_map/sum_branch/pallas_call | solution.py:112
  245.3 25.8 %gather_two.1 = bf16[4,128,2048]{2,1,0:T(8,128)(2,1)} custom-call(bf16[128,2048]{1,0:T(8,128)(2,1)} %multiply_convert_fusion.4.refs_0_), custom_call_target="tpu_custom_call" | custom-call | tf_op jit(solution)/shard_map/gather_two/pallas_call | solution.py:112
  271.1 10.3 %fusion.82 = f32[512,2816]{1,0:T(8,128)S(1)} fusion(bf16[512,2048]{1,0:T(8,128)(2,1)} %bitcast.238, bf16[2048,2816]{1,0:T(8,128)(2,1)} %bitcast.271), kind=kOutput, calls=%fused_computation.227 | convolution fusion | flops 5905580032 | bytes 19398656 | tf_op jit(solution)/shard_map/dot_general | solution.py:487
  281.5 8.4 %multiply_convert_fusion.2 = (bf16[512,1408]{1,0:T(8,128)(2,1)S(1)}, bf16[512,1408]{1,0:T(8,128)(2,1)S(1)}, bf16[512,1408]{1,0:T(8,128)(2,1)}) fusion(f32[512,2816]{1,0:T(8,128)S(1)} %fusion.82, bf16[512,2048]{1,0:T(8,128)(2,1)S(1)} %bitcast.279, bf16[2048,1408]{1,0:T(8,128)(2,1)} %bitcast.275), kind=kOutput, calls=%fused_computation.38 | convolution fusion | flops 2963603456 | bytes 17956864 | tf_op jit(solution)/shard_map/dot_general | solution.py:487
  289.9 7.4 %convolution_convert_fusion.4 = bf16[512,2048]{1,0:T(8,128)(2,1)} fusion(bf16[2048,2816]{1,0:T(8,128)(2,1)S(1)} %bitcast.274, bf16[512,1408]{1,0:T(8,128)(2,1)S(1)} %get-tuple-element.75, bf16[512,1408]{1,0:T(8,128)(2,1)S(1)} %get-tuple-element.74), kind=kOutput, calls=%fused_computation.32 | convolution fusion | flops 5912395776 | bytes 16515072 | tf_op jit(solution)/shard_map/dot_general | solution.py:487
  297.3 24.9 %sum_grad_two.1 = bf16[3,128,2048]{2,1,0:T(8,128)(2,1)} custom-call(bf16[4,128,2048]{2,1,0:T(8,128)(2,1)} %bitcast.223), custom_call_target="tpu_custom_call" | custom-call | tf_op jit(solution)/shard_map/sum_grad_two/pallas_call | solution.py:112
  327.0 7.4 %convolution_convert_fusion.7 = bf16[512,2048]{1,0:T(8,128)(2,1)} fusion(bf16[512,1408]{1,0:T(8,128)(2,1)S(1)} %copy-done.67, bf16[2048,1408]{1,0:T(8,128)(2,1)} %bitcast.276), kind=kOutput, calls=%fused_computation.35 | convolution fusion | flops 2953838592 | bytes 9306112 | tf_op jit(solution)/shard_map/dot_general | solution.py:487
  334.3 24.0 %sum_outputs.1 = bf16[3,128,2048]{2,1,0:T(8,128)(2,1)} custom-call(bf16[4,128,2048]{2,1,0:T(8,128)(2,1)} %bitcast.234), custom_call_target="tpu_custom_call" | custom-call | tf_op jit(solution)/shard_map/sum_outputs/pallas_call | solution.py:112
  363.2 23.0 %gather_branch.1 = bf16[4,128,2048]{2,1,0:T(8,128)(2,1)} custom-call(bf16[128,2048]{1,0:T(8,128)(2,1)} %get-tuple-element.70.refs_0_), custom_call_target="tpu_custom_call" | custom-call | tf_op jit(solution)/shard_map/gather_branch/pallas_call | solution.py:112
  386.3 3.7 convolution_convert_fusion.8
  390.0 8.6 %fusion.21 = f32[1024,64]{0,1:T(8,128)S(1)} fusion(bf16[512,8,64]{0,2,1:T(8,128)(2,1)S(1)} %bitcast.236, f32[8,512,1024]{1,2,0:T(8,128)} %get-tuple-element.107, f32[8,512]{1,0:T(8,128)S(1)} %log_add_fusion), kind=kOutput, calls=%fused_computation.67 | convolution fusion | flops 545259520 | bytes 17580032 | tf_op jit(solution)/shard_map/hqk,qhd->kd/dot_general | solution.py:584
  399.5 8.3 %fusion = (f32[8,512]{1,0:T(8,128)S(1)}, f32[1024,512,8]{1,0,2:T(8,128)}) fusion(f32[8,512,1024]{1,2,0:T(8,128)S(1)} %bitcast.214, f32[8,512]{1,0:T(8,128)S(1)} %log_add_fusion, bf16[512,8,64]{0,2,1:T(8,128)(2,1)S(1)} %bitcast.237, bf16[512,128]{1,0:T(8,128)(2,1)S(1)} %get-tuple-element.94, bf16[512,128]{1,0:T(8,128)(2,1)S(1)} %get-tuple-element.93), kind=kOutput, calls=%fused_computation.2 | convolution fusion | flops 549711872 | bytes 34373632 | tf_op jit(solution)/shard_map/qhd,kd->hqk/dot_general | solution.py:579
  407.8 7.8 %fusion.2 = bf16[8,512,1024]{1,2,0:T(8,128)(2,1)S(1)} fusion(f32[1024,512,8]{1,0,2:T(8,128)} %get-tuple-element.109, f32[8,512,1024]{1,2,0:T(8,128)S(1)} %bitcast.214, f32[8,512]{1,0:T(8,128)S(1)} %get-tuple-element.108, f32[8,512]{1,0:T(8,128)S(1)} %log_add_fusion), kind=kLoop, calls=%fused_computation.4 | loop fusion | flops 16777216 | bytes 41975808 | tf_op jit(solution)/shard_map/convert_element_type | solution.py:581
  419.8 5.3 swap_grad_keys.1
  427.8 5.0 fusion.16
  434.6 3.2 convolution_convert_fusion.6
  437.8 21.0 %sum_grad_one.1 = bf16[3,128,2048]{2,1,0:T(8,128)(2,1)} custom-call(bf16[4,128,2048]{2,1,0:T(8,128)(2,1)} %bitcast.226), custom_call_target="tpu_custom_call" | custom-call | tf_op jit(solution)/shard_map/sum_grad_one/pallas_call | solution.py:112
  463.5 3.4 convolution_convert_fusion.2
  467.0 9.2 %convolution_convert_fusion = bf16[2048,2816]{1,0:T(8,128)(2,1)} fusion(bf16[512,2048]{1,0:T(8,128)(2,1)S(1)} %bitcast.239, bf16[512,1408]{1,0:T(8,128)(2,1)S(1)} %copy-done.72, bf16[512,1408]{1,0:T(8,128)(2,1)S(1)} %copy-done.70), kind=kOutput, calls=%fused_computation.13 | convolution fusion | flops 5917114368 | bytes 16515072 | tf_op jit(solution)/shard_map/dot_general | solution.py:487
  476.2 5.3 convolution_convert_fusion.1
  484.1 17.7 %grads_core.1 = (bf16[4,2,128,640]{3,2,1,0:T(8,128)(2,1)}, bf16[4,2,128,2816]{3,2,1,0:T(8,128)(2,1)}, bf16[4,2,128,1408]{3,2,1,0:T(8,128)(2,1)}, bf16[2,2,4,16,2048]{4,3,2,1,0:T(8,128)(2,1)}) custom-call(bf16[4,2,2,128,640]{4,3,2,1,0:T(8,128)(2,1)} %bitcast.221, bf16[4,2,2,128,2816]{4,3,2,1,0:T(8,128)(2,1)} %bitcast.215, ...), custom_call_target="tpu_custom_call" | custom-call | tf_op jit(solution)/shard_map/grads_core/pallas_call | solution.py:112
  504.7 8.3 %fusion.5.refs_1_ = bf16[4,2,128,2816]{3,2,1,0:T(8,128)(2,1)} fusion(bf16[4,2,128,2816]{3,2,1,0:T(8,128)(2,1)} %get-tuple-element.47, bf16[4,2,2,128,2816]{4,3,2,1,0:T(8,128)(2,1)} %bitcast.216, s32[]{:T(128)S(6)} %select_n.137), kind=kLoop, calls=%fused_computation.12 | loop fusion | flops 11534336 | bytes 17301508 | tf_op jit(solution)/shard_map/convert_element_type | solution.py:433
  516.9 64.0 %grads_first.1 = (bf16[3,2,128,384]{3,2,1,0:T(8,128)(2,1)}, bf16[3,4,64,256]{3,2,1,0:T(8,128)(2,1)}, bf16[3,2,128,1408]{3,2,1,0:T(8,128)(2,1)}, bf16[3,4,64,1408...) custom-call(bf16[4,2,128,640]{3,2,1,0:T(8,128)(2,1)} %fusion.13.refs, ...), custom_call_target="tpu_custom_call" | custom-call | tf_op jit(solution)/shard_map/grads_first/pallas_call | solution.py:112
  599.2 19.0 %grads_second.1 = (bf16[3,64,384]{2,1,0:T(8,128)(2,1)}, bf16[3,64,256]{2,1,0:T(8,128)(2,1)}, bf16[3,64,1408]{2,1,0:T(8,128)(2,1)}, bf16[3,64,1408]{2,1,0:T(8,128...) custom-call(bf16[2,128,384]{2,1,0:T(8,128)(2,1)} %add_convert_fusion, ...), custom_call_target="tpu_custom_call" | custom-call | tf_op jit(solution)/shard_map/grads_second/pallas_call | solution.py:112
  631.5 13.1 %grads_y.1 = (bf16[4,16,640]{2,1,0:T(8,128)(2,1)}, bf16[4,16,2816]{2,1,0:T(8,128)(2,1)}, bf16[4,16,1408]{2,1,0:T(8,128)(2,1)}, bf16[16,2048]{1,0:T(8,128)(2,1)}) custom-call(bf16[4,16,640]{2,1,0:T(8,128)(2,1)} %pad_maximum_fusion.15.refs_0_, bf16[4,16,2816]{2,1,0:T(8,128)(2,1)} %pad_maximum_fusion.7.refs_1_, ...), custom_call_target="tpu_custom_call" | custom-call | tf_op jit(solution)/shard_map/grads_y/pallas_call | solution.py:112
  (306 shorter events, 100.9 us)
Async XLA Ops:
  57.3 99.6 %copy-start.55 = (f32[16]{0:T(128)}, f32[16]{0:T(128)S(1)}, u32[]{:S(2)}) copy-start(f32[16]{0:T(128)S(1)} %convert_element_type.402) | copy-start | bytes 196
  58.2 98.7 %copy-start.53 = (f32[16]{0:T(128)}, f32[16]{0:T(128)S(1)}, u32[]{:S(2)}) copy-start(f32[16]{0:T(128)S(1)} %convert_element_type.405) | copy-start | bytes 196
  166.0 20.0 %copy-start.23 = (bf16[512,8,32]{0,2,1:T(8,128)(2,1)}, bf16[512,8,32]{0,2,1:T(8,128)(2,1)S(1)}, u32[]{:S(2)}) copy-start(bf16[512,8,32]{0,2,1:T(8,128)(2,1)S(1)} %get-tuple-element.79) | copy-start | bytes 786436
  166.1 20.0 %copy-start.25 = (bf16[512,8,32]{0,2,1:T(8,128)(2,1)}, bf16[512,8,32]{0,2,1:T(8,128)(2,1)S(1)}, u32[]{:S(2)}) copy-start(bf16[512,8,32]{0,2,1:T(8,128)(2,1)S(1)} %get-tuple-element.80) | copy-start | bytes 786436
  194.1 7.9 %copy-start.43 = (f32[8,512]{1,0:T(8,128)}, f32[8,512]{1,0:T(8,128)S(1)}, u32[]{:S(2)}) copy-start(f32[8,512]{1,0:T(8,128)S(1)} %fusion.3) | copy-start | bytes 49156
  194.1 7.9 %copy-start.62 = (bf16[2,2,2,4,16,2048]{5,4,3,2,1,0:T(8,128)(2,1)S(1)}, bf16[2,2,2,4,16,2048]{5,4,3,2,1,0:T(8,128)(2,1)}, u32[]{:S(2)}) copy-start(bf16[2,2,2,4,16,2048]{5,4,3,2,1,0:T(8,128)(2,1)} %get-tuple-element.42) | copy-start | bytes 6291460
  271.1 10.3 %copy-start.60 = (bf16[4,128,2048]{2,1,0:T(8,128)(2,1)S(1)}, bf16[4,128,2048]{2,1,0:T(8,128)(2,1)}, u32[]{:S(2)}) copy-start(bf16[4,128,2048]{2,1,0:T(8,128)(2,1)} %get-tuple-element.45) | copy-start | bytes 6291460
  271.1 18.7 %slice-start.6 = ((s8[11534336]{0:T(1024)(128)(4,1)}), s8[4194304]{0:T(1024)(128)(4,1)S(1)}, s32[]{:S(2)}) async-start(s8[11534336]{0:T(1024)(128)(4,1)} %bitcast.272), calls=%async_computation.6 | async-start | bytes 8388608
  271.1 18.7 %slice-start.7 = ((s8[11534336]{0:T(1024)(128)(4,1)}), s8[4194304]{0:T(1024)(128)(4,1)S(1)}, s32[]{:S(2)}) async-start(s8[11534336]{0:T(1024)(128)(4,1)} %bitcast.272), calls=%async_computation.7 | async-start | bytes 8388608
  281.4 8.4 %slice-start.8 = ((s8[11534336]{0:T(1024)(128)(4,1)}), s8[3145728]{0:T(1024)(128)(4,1)S(1)}, s32[]{:S(2)}) async-start(s8[11534336]{0:T(1024)(128)(4,1)} %bitcast.272), calls=%async_computation.8 | async-start | bytes 6291456
  289.9 7.4 %copy-start.69 = (bf16[512,1408]{1,0:T(8,128)(2,1)}, bf16[512,1408]{1,0:T(8,128)(2,1)S(1)}, u32[]{:S(2)}) copy-start(bf16[512,1408]{1,0:T(8,128)(2,1)S(1)} %get-tuple-element.74) | copy-start | bytes 4325380
  289.9 7.4 %copy-start.71 = (bf16[512,1408]{1,0:T(8,128)(2,1)}, bf16[512,1408]{1,0:T(8,128)(2,1)S(1)}, u32[]{:S(2)}) copy-start(bf16[512,1408]{1,0:T(8,128)(2,1)S(1)} %get-tuple-element.75) | copy-start | bytes 4325380
  386.3 12.3 %slice-start = ((s8[16777216]{0:T(1024)(128)(4,1)}), s8[4194304]{0:T(1024)(128)(4,1)S(1)}, s32[]{:S(2)}) async-start(s8[16777216]{0:T(1024)(128)(4,1)} %bitcast.213), calls=%async_computation | async-start | bytes 8388608
  390.0 8.6 %slice-start.1 = ((s8[16777216]{0:T(1024)(128)(4,1)}), s8[4194304]{0:T(1024)(128)(4,1)S(1)}, s32[]{:S(2)}) async-start(s8[16777216]{0:T(1024)(128)(4,1)} %bitcast.213), calls=%async_computation.1 | async-start | bytes 8388608
  390.0 8.6 %slice-start.2 = ((s8[16777216]{0:T(1024)(128)(4,1)}), s8[4194304]{0:T(1024)(128)(4,1)S(1)}, s32[]{:S(2)}) async-start(s8[16777216]{0:T(1024)(128)(4,1)} %bitcast.213), calls=%async_computation.2 | async-start | bytes 8388608
  390.0 9.4 %slice-start.3 = ((s8[16777216]{0:T(1024)(128)(4,1)}), s8[4194304]{0:T(1024)(128)(4,1)S(1)}, s32[]{:S(2)}) async-start(s8[16777216]{0:T(1024)(128)(4,1)} %bitcast.213), calls=%async_computation.3 | async-start | bytes 8388608
  407.7 7.9 %copy-start.24 = (bf16[512,8,32]{0,2,1:T(8,128)(2,1)S(1)}, bf16[512,8,32]{0,2,1:T(8,128)(2,1)}, u32[]{:S(2)}) copy-start(bf16[512,8,32]{0,2,1:T(8,128)(2,1)} %copy-done.23) | copy-start | bytes 786436
  407.8 7.9 %copy-start.26 = (bf16[512,8,32]{0,2,1:T(8,128)(2,1)S(1)}, bf16[512,8,32]{0,2,1:T(8,128)(2,1)}, u32[]{:S(2)}) copy-start(bf16[512,8,32]{0,2,1:T(8,128)(2,1)} %copy-done.25) | copy-start | bytes 786436
  418.9 7.4 %copy-start.46 = (f32[512]{0:T(512)S(1)}, f32[512]{0:T(512)}, u32[]{:S(2)}) copy-start(f32[512]{0:T(512)} %copy-done.45) | copy-start | bytes 6148
  418.9 7.5 %copy-start.49 = (f32[32]{0:T(128)S(1)}, f32[32]{0:T(128)}, u32[]{:S(2)}) copy-start(f32[32]{0:T(128)} %copy-done.48) | copy-start | bytes 388
  437.8 23.0 %copy-start.57 = (f32[128]{0:T(128)S(1)}, f32[128]{0:T(128)}, u32[]{:S(2)}) copy-start(f32[128]{0:T(128)} %get-tuple-element.86) | copy-start | bytes 1540
  437.8 23.0 %copy-start.5 = (bf16[128,2048]{1,0:T(8,128)(2,1)S(1)}, bf16[128,2048]{1,0:T(8,128)(2,1)}, u32[]{:S(2)}) copy-start(bf16[128,2048]{1,0:T(8,128)(2,1)} %refs_0_.1) | copy-start | bytes 1572868
  466.9 9.2 %copy-start.61 = (bf16[4,128,2048]{2,1,0:T(8,128)(2,1)S(1)}, bf16[4,128,2048]{2,1,0:T(8,128)(2,1)}, u32[]{:S(2)}) copy-start(bf16[4,128,2048]{2,1,0:T(8,128)(2,1)} %get-tuple-element.45) | copy-start | bytes 6291460
  467.0 9.2 %copy-start.68 = (bf16[512,1408]{1,0:T(8,128)(2,1)S(1)}, bf16[512,1408]{1,0:T(8,128)(2,1)}, u32[]{:S(2)}) copy-start(bf16[512,1408]{1,0:T(8,128)(2,1)} %get-tuple-element.76) | copy-start | bytes 4325380
  484.1 17.8 %copy-start.8 = (bf16[2048,640]{1,0:T(8,128)(2,1)S(1)}, bf16[2048,640]{1,0:T(8,128)(2,1)}, u32[]{:S(2)}) copy-start(bf16[2048,640]{1,0:T(8,128)(2,1)} %convolution_convert_fusion.2) | copy-start | bytes 7864324
  501.9 11.2 %slice-start.4 = ((s8[5767168]{0:T(1024)(128)(4,1)}), s8[4194304]{0:T(1024)(128)(4,1)S(1)}, s32[]{:S(2)}) async-start(s8[5767168]{0:T(1024)(128)(4,1)} %bitcast.218), calls=%async_computation.4 | async-start | bytes 8388608
  504.7 8.3 %slice-start.5 = ((s8[5767168]{0:T(1024)(128)(4,1)}), s8[1572864]{0:T(1024)(128)(4,1)S(1)}, s32[]{:S(2)}) async-start(s8[5767168]{0:T(1024)(128)(4,1)} %bitcast.218), calls=%async_computation.5 | async-start | bytes 3145728
  504.7 8.3 %copy-start.14 = (bf16[4,2,128,1408]{3,2,1,0:T(8,128)(2,1)S(1)}, bf16[4,2,128,1408]{3,2,1,0:T(8,128)(2,1)}, u32[]{:S(2)}) copy-start(bf16[4,2,128,1408]{3,2,1,0:T(8,128)(2,1)} %get-tuple-element.48) | copy-start | bytes 8650756
  516.9 66.1 %copy-start.6 = (bf16[4,2,128,640]{3,2,1,0:T(8,128)(2,1)S(1)}, bf16[4,2,128,640]{3,2,1,0:T(8,128)(2,1)}, u32[]{:S(2)}) copy-start(bf16[4,2,128,640]{3,2,1,0:T(8,128)(2,1)} %fusion.13.refs_0_) | copy-start | bytes 3932164
  581.0 7.4 %copy-start.16 = (bf16[3,2,128,1408]{3,2,1,0:T(8,128)(2,1)S(1)}, bf16[3,2,128,1408]{3,2,1,0:T(8,128)(2,1)}, u32[]{:S(2)}) copy-start(bf16[3,2,128,1408]{3,2,1,0:T(8,128)(2,1)} %get-tuple-element.52) | copy-start | bytes 6488068
  626.6 19.3 %copy-start.29 = (bf16[16,2560]{1,0:T(8,128)(2,1)S(1)}, bf16[16,2560]{1,0:T(8,128)(2,1)}, u32[]{:S(2)}) copy-start(bf16[16,2560]{1,0:T(8,128)(2,1)} %param.11) | copy-start | bytes 245764
  626.6 19.3 %copy-start.56 = (f32[16]{0:T(128)S(1)}, f32[16]{0:T(128)}, u32[]{:S(2)}) copy-start(f32[16]{0:T(128)} %copy-done.55) | copy-start | bytes 196
  (50 other events, 144.6 us)

commit v2 on v1

--- a/solution.py
+++ b/solution.py
@@ -27,6 +27,11 @@
 
 SPLITS = ((PROJ, 384), (2 * HID, HID), (HID, 640))
 OUT_SPLIT = 1024
+VMEM_LIMIT = 60 << 20
+
+NN = ((1,), (0,))
+NT = ((1,), (1,))
+TN = ((0,), (0,))
 
 
 def place():
@@ -128,74 +133,315 @@
     return jax.ShapeDtypeStruct(shape, dtype)
 
 
-def ring_gather(parts, ident, name):
-    n = len(parts)
-
-    def kernel(*refs):
-        ins, outs, (send, recv, local) = refs[:n], refs[n : 2 * n], refs[2 * n :]
-        xh, xl, y, z, c = place()
-        greet([along_y(d) for d in (1, 2, 3)], False)
+class RingGather:
+    def __init__(self, copy, own, dst, y):
+        half = dst.shape[2] // 2
+        lo, hi = pl.ds(0, half), pl.ds(half, half)
+        back, on = (y + 3) % 4, (y + 1) % 4
+
+        def first(cols, to):
+            return copy(own.at[:, cols], dst.at[y, :, cols], to)
+
+        def one(slot, cols, to):
+            at = dst.at[slot, :, cols]
+            return copy(at, at, to)
+
+        self.first = [first(lo, along_y(1)), first(hi, along_y(3)), first(hi, along_y(1)), first(lo, along_y(3))]
+        self.second = [one(back, lo, along_y(1)), one(on, hi, along_y(3))]
+
+    def start(self):
+        for cp in self.first:
+            cp.start()
+
+    def turn(self):
+        for got, cp in zip(self.first, self.second):
+            got.wait_recv()
+            cp.start()
+
+    def near(self):
+        for cp in self.first[2:]:
+            cp.wait_recv()
+
+    def far(self):
+        for cp in self.second:
+            cp.wait_recv()
+
+    def sent(self):
+        for cp in self.first + self.second:
+            cp.wait_send()
+
+
+class RingSum:
+    def __init__(self, copy, part, halves, whole, y):
+        half = part.shape[2] // 2
+        lo, hi = pl.ds(0, half), pl.ds(half, half)
+        self.part, self.halves, self.whole, self.y = part, halves, whole, y
+        self.cols = (lo, hi)
+        far, on, back = (y + 2) % 4, (y + 1) % 4, (y + 3) % 4
+        self.far = [
+            copy(part.at[far, :, lo], halves.at[0], along_y(1)),
+            copy(part.at[far, :, hi], halves.at[1], along_y(3)),
+        ]
+        self.near = [
+            copy(part.at[on, :, hi], whole.at[0, :, hi], along_y(1)),
+            copy(part.at[back, :, lo], whole.at[1, :, lo], along_y(3)),
+        ]
+        self.last = [
+            copy(part.at[on, :, lo], whole.at[0, :, lo], along_y(1)),
+            copy(part.at[back, :, hi], whole.at[1, :, hi], along_y(3)),
+        ]
+        self.slots = (on, back)
+
+    def start(self):
+        for cp in self.far + self.near:
+            cp.start()
+
+    def turn(self):
+        for k in range(2):
+            self.far[k].wait_recv()
+            slot, cols = self.slots[k], self.cols[k]
+
+            def body(r, _, slot=slot, cols=cols, k=k):
+                rows = pl.ds(r * 32, 32)
+                both = self.part[slot, rows, cols].astype(F32) + self.halves[k, rows].astype(F32)
+                self.part[slot, rows, cols] = both.astype(BF16)
+                return 0
+
+            lax.fori_loop(0, self.part.shape[1] // 32, body, 0)
+            self.last[k].start()
+
+    def finish(self):
+        for cp in self.near + self.last:
+            cp.wait_recv()
+
+    def rows(self, rows):
+        own = self.part[self.y, rows].astype(F32)
+        return own + self.whole[0, rows].astype(F32) + self.whole[1, rows].astype(F32)
+
+    def sent(self):
+        for cp in self.far + self.near + self.last:
+            cp.wait_send()
+
+
+def ring_sum(part, ident, name):
+    rows, cols = part.shape[0] // 4, part.shape[1]
+
+    def kernel(src, dst, work, halves, whole, send, recv, local):
+        y = place()[2]
+        load = pltpu.make_async_copy(src, work, local.at[0])
+        load.start()
+        greet([along_y(1), along_y(3)], False)
+        load.wait()
+        ring = RingSum(Copies(send, recv), work, halves, whole, y)
+        ring.start()
+        ring.turn()
+        ring.finish()
+
+        def body(r, _):
+            at = pl.ds(r * 32, 32)
+            dst[at] = ring.rows(at)
+            return 0
+
+        lax.fori_loop(0, rows // 32, body, 0)
+        ring.sent()
+
+    return pl.pallas_call(
+        kernel,
+        out_shape=struct((rows, cols), F32),
+        in_specs=[pl.BlockSpec(memory_space=pl.ANY)],
+        out_specs=pl.BlockSpec(memory_space=pltpu.VMEM),
+        scratch_shapes=[
+            pltpu.VMEM((4, rows, cols), BF16),
+            pltpu.VMEM((2, rows, cols // 2), BF16),
+            pltpu.VMEM((2, rows, cols), BF16),
+            pltpu.SemaphoreType.DMA((6,)),
+            pltpu.SemaphoreType.DMA((6,)),
+            pltpu.SemaphoreType.DMA((1,)),
+        ],
+        name=name,
+        compiler_params=pltpu.CompilerParams(
+            collective_id=ident, has_side_effects=True, vmem_limit_bytes=VMEM_LIMIT
+        ),
+    )(part.reshape(4, rows, cols))
+
+
+def ring_gather(part, ident, name):
+    def kernel(src, dst, send, recv, local):
+        y = place()[2]
+        own = pltpu.make_async_copy(src, dst.at[y], local.at[0])
+        own.start()
+        greet([along_y(1), along_y(3)], False)
+        ring = RingGather(Copies(send, recv), src, dst, y)
+        ring.start()
+        ring.turn()
+        ring.near()
+        ring.far()
+        ring.sent()
+        own.wait()
+
+    return pl.pallas_call(
+        kernel,
+        out_shape=struct((4,) + part.shape, part.dtype),
+        in_specs=[pl.BlockSpec(memory_space=pltpu.VMEM)],
+        out_specs=pl.BlockSpec(memory_space=pl.ANY),
+        scratch_shapes=[
+            pltpu.SemaphoreType.DMA((6,)),
+            pltpu.SemaphoreType.DMA((6,)),
+            pltpu.SemaphoreType.DMA((1,)),
+        ],
+        name=name,
+        compiler_params=pltpu.CompilerParams(collective_id=ident, has_side_effects=True),
+    )(part)
+
+
+class Gather:
+    def __init__(self, copy, out, a, at, rows_only=False):
+        xh, xl, y, z, c = at
+        cols = out.shape[-1]
+        left, right = pl.ds(0, a), pl.ds(a, cols - a)
+        def cut(half, n):
+            return slice(None) if half is None else pl.ds(half * (n // 2), n // 2)
+
+        if rows_only:
+            block = lambda z, x, c, cols: out.at[x[0], c, x[1], z, :, cols]
+            z_line = lambda x, c, cols, half: out.at[x[0], c, x[1], cut(half, 4), :, cols]
+            x_line = lambda z, c, cols, half: out.at[cut(half, 2), c, :, z, :, cols]
+        else:
+            block = lambda z, x, c, cols: out.at[z, x[0], c, pl.ds(x[1] * 64, 64), cols]
+            z_line = lambda x, c, cols, half: out.at[cut(half, 4), x[0], c, pl.ds(x[1] * 64, 64), cols]
+            x_line = lambda z, c, cols, half: out.at[z, cut(half, 2), c, :, cols]
+
+        def same(ref, to):
+            return copy(ref, ref, to)
+
+        here = (xh, xl)
+        self.first = []
+        for d in (1, 3, 2):
+            self.first.append(same(block(z, here, c, left), along_x(d)))
+            self.first.append(same(block(z, here, c, right), along_z(d)))
+        a_lo, a_hi = lambda z: x_line(z, c, left, 0), lambda z: x_line(z, c, left, 1)
+        b_lo, b_hi = lambda x: z_line(x, c, right, 0), lambda x: z_line(x, c, right, 1)
+        z_at = [(z + d) % 4 for d in range(4)]
+        x_at = [along_x(d)(*at)[:2] for d in range(4)]
+        self.lines = []
+        for lo, hi, spots, along in ((a_lo, a_hi, z_at, along_z), (b_lo, b_hi, x_at, along_x)):
+            going = [
+                same(lo(spots[0]), along(1)),
+                same(hi(spots[0]), along(3)),
+                same(hi(spots[0]), along(1)),
+                same(lo(spots[0]), along(3)),
+            ]
+            on = [same(lo(spots[3]), along(1)), same(hi(spots[1]), along(3))]
+            self.lines.append((going, on))
+        self.core = [same(block(z, here, c, pl.ds(0, cols)), sibling)]
+        for d in (1, 3, 2):
+            self.core.append(same(block(z, x_at[d], c, left), sibling))
+            self.core.append(same(block(z_at[d], here, c, right), sibling))
+        self.core_lines = []
+        for d in (3, 1, 2):
+            self.core_lines.append(
+                (same(x_line(z_at[d], c, left, None), sibling), same(z_line(x_at[d], c, right, None), sibling))
+            )
+
+    def start(self):
+        for cp in self.first:
+            cp.start()
+        self.core[0].start()
+
+    def turn(self):
+        for cp in self.first:
+            cp.wait_recv()
+        for going, _ in self.lines:
+            for cp in going:
+                cp.start()
+        for cp in self.core[1:]:
+            cp.start()
+
+    def pass_on(self):
+        for going, on in self.lines:
+            for got, cp in zip(going[:2], on):
+                got.wait_recv()
+                cp.start()
+
+    def near(self):
+        for k, (going, _) in enumerate(self.lines):
+            for side in range(2):
+                going[2 + side].wait_recv()
+                self.core_lines[side][k].start()
+
+    def far(self):
+        for k, (_, on) in enumerate(self.lines):
+            for cp in on:
+                cp.wait_recv()
+            self.core_lines[2][k].start()
+
+    def finish(self):
+        for cp in self.core + [cp for pair in self.core_lines for cp in pair]:
+            cp.wait_recv()
+
+    def sent(self):
+        for going, on in self.lines:
+            for cp in going + on:
+                cp.wait_send()
+        for cp in self.first + self.core + [cp for pair in self.core_lines for cp in pair]:
+            cp.wait_send()
+
+
+def dot(left, right, dims=((1,), (0,))):
+    return lax.dot_general(left, right, (dims, ((), ())), preferred_element_type=F32)
+
+
+def swap_halves(v):
+    lane = lax.broadcasted_iota(jnp.int32, v.shape, 1)
+    return jnp.where(lane % 64 < 32, pltpu.roll(v, 96, 1), pltpu.roll(v, 32, 1))
+
+
+def forward_attention(tokens, cotangent, spots, freqs, w_proj, w_gu, w_down, out_rows, ident):
+    rows = tokens.shape[0]
+    count = 4 * rows
+    groups = [w_proj, w_gu, w_down]
+
+    def kernel(
+        tok_ref, cot_ref, spot_ref, freq_ref, wp, wg, wd, wo,
+        normed_out, cot_all, gp, gg, gd, go, q_out, kv_out, att_out, lse_out, spot_out, middle_out, two_all,
+        tok, normed, wp_v, wo_v, q_s, kv, vx, bias, att, part, halves, whole, spot_all, own_two, send, recv, local,
+    ):
+        at = place()
+        xh, xl, y, z, c = at
         copy = Copies(send, recv)
-        going = []
-        for i, o in zip(ins, outs):
-            for d in (1, 3, 2):
-                going.append(copy(i, o.at[y], along_y(d)))
-                going[-1].start()
-        own = [pltpu.make_async_copy(i, o.at[y], local.at[k]) for k, (i, o) in enumerate(zip(ins, outs))]
-        for cp in own:
+        slot = pl.ds(xl * 64 + y * 16, 16)
+        nlocal = [0]
+
+        def near(src, dst):
+            cp = pltpu.make_async_copy(src, dst, local.at[nlocal[0]])
+            nlocal[0] += 1
+            return cp
+
+        to_y = []
+        stay = []
+        for i, o in ((wp, gp), (wg, gg), (wd, gd)):
+            to_y.append([copy(i.at[(y + d) % 4], o.at[z, xh, c, slot], along_y(d)) for d in (1, 3, 2)])
+            stay.append(near(i.at[y], o.at[z, xh, c, slot]))
+        over = copy(wo, go.at[xh, c, xl, y], crossed)
+        keep = near(wo, go.at[xh, c, xl, z])
+        spot_copies = [copy(spot_all.at[y], spot_all.at[y], along_y(d)) for d in (1, 3, 2)]
+        tok_ring = RingGather(copy, tok_ref, tok, y)
+        cot_ring = RingGather(copy, cot_ref, cot_all, y)
+        two_ring = RingGather(copy, own_two, two_all, y)
+        branch = RingSum(copy, part, halves, whole, y)
+        kv_copy = copy(kv.at[1], kv.at[0], half_partner)
+        g_proj = Gather(copy, gp, SPLITS[0][1], at)
+        g_gu = Gather(copy, gg, SPLITS[1][1], at)
+        g_down = Gather(copy, gd, SPLITS[2][1], at)
+        g_out = Gather(copy, go, OUT_SPLIT, at, True)
+
+        cot_own = near(cot_ref, cot_all.at[y])
+        tok_own = near(tok_ref, tok.at[y])
+        tok_own.start()
+        cot_own.start()
+        spot_all[y] = spot_ref[...]
+        for cp in stay:
             cp.start()
-        for cp in going:
-            cp.wait()
-        for cp in own:
-            cp.wait()
-
-    return comm_call(
-        kernel, name, ident, parts, [struct((4,) + p.shape, p.dtype) for p in parts], 3 * n, n
-    )
-
-
-def ring_scatter(part, ident, name):
-    def kernel(src, dst, send, recv, local):
-        xh, xl, y, z, c = place()
-        greet([along_y(d) for d in (1, 2, 3)], False)
-        copy = Copies(send, recv)
-        going = []
-        for d in (1, 3, 2):
-            going.append(copy(src.at[(y + d) % 4], dst.at[d - 1], along_y(d)))
-            going[-1].start()
-        for cp in going:
-            cp.wait()
-
-    (out,) = comm_call(kernel, name, ident, [part], [struct((3,) + part.shape[1:])], 3)
-    return out
-
-
-def ring_sum(part, ident, name):
-    part = part.reshape(4, part.shape[0] // 4, part.shape[1])
-    own = lax.dynamic_index_in_dim(part, lax.axis_index("ctx") % 4, 0, keepdims=False)
-    others = ring_scatter(part, ident, name)
-    return own.astype(F32) + jnp.sum(others.astype(F32), 0)
-
-
-def swap(part, to, ident, name):
-    def kernel(src, dst, send, recv, local):
-        greet([to], False)
-        cp = Copies(send, recv)(src, dst, to)
-        cp.start()
-        cp.wait()
-
-    (out,) = comm_call(kernel, name, ident, [part], [struct(part.shape, part.dtype)], 1)
-    return out
-
-
-def gather_weights(blocks, out_rows, ident):
-    n = len(blocks)
-
-    def kernel(*refs):
-        ins, rows_in = refs[:n], refs[n]
-        outs, rows_out = refs[n + 1 : 2 * n + 1], refs[2 * n + 1]
-        send, recv, local = refs[2 * n + 2 :]
-        xh, xl, y, z, c = place()
         greet(
             [along_y(d) for d in (1, 2, 3)]
             + [along_x(d) for d in (1, 2, 3)]
@@ -203,129 +449,267 @@
             + [sibling],
             True,
         )
-        copy = Copies(send, recv)
-        mine = pl.ds(xl * 64, 64)
-        slot = pl.ds(xl * 64 + y * 16, 16)
-        started = []
-
-        def go(src, dst, to):
-            cp = copy(src, dst, to)
+        away = y != z
+        for cp in to_y[0]:
             cp.start()
-            started.append(cp)
-            return cp
-
-        first = []
-        for i, o in zip(ins, outs):
-            for d in (1, 3, 2):
-                first.append(go(i.at[(y + d) % 4], o.at[z, xh, c, slot], along_y(d)))
-        over = copy(rows_in, rows_out.at[xh, c, xl, y], crossed)
-        away = y != z
 
         @pl.when(away)
         def _():
             over.start()
 
-        own = [
-            pltpu.make_async_copy(i.at[y], o.at[z, xh, c, slot], local.at[k])
-            for k, (i, o) in enumerate(zip(ins, outs))
-        ]
-        for cp in own:
-            cp.start()
-        stay = pltpu.make_async_copy(rows_in, rows_out.at[xh, c, xl, z], local.at[n])
-
         @pl.when(jnp.logical_not(away))
         def _():
-            stay.start()
-            stay.wait()
-
-        for cp in own:
-            cp.wait()
-        for cp in first:
+            keep.start()
+
+        tok_ring.start()
+        for cp in spot_copies + to_y[1] + to_y[2]:
+            cp.start()
+
+        def norm_block(k):
+            def body(r, _):
+                rs = pl.ds(r * 32, 32)
+                v = tok[k, rs].astype(F32)
+                inv = lax.rsqrt(jnp.mean(v * v, -1, keepdims=True) + EPS)
+                normed[k, rs] = (v * inv).astype(BF16)
+                return 0
+
+            lax.fori_loop(0, rows // 32, body, 0)
+
+        stay[0].wait()
+        for cp in to_y[0]:
             cp.wait_recv()
+        g_proj.start()
 
         @pl.when(away)
         def _():
             over.wait()
 
-        a_first, b_first = [], []
-        for o, (cols, a) in zip(outs, SPLITS):
-            left, right = pl.ds(0, a), pl.ds(a, cols - a)
-            for d in (1, 3, 2):
-                a_first.append(go(o.at[z, xh, c, mine, left], o.at[z, xh, c, mine, left], along_x(d)))
-                b_first.append(go(o.at[z, xh, c, mine, right], o.at[z, xh, c, mine, right], along_z(d)))
-        left, right = pl.ds(0, OUT_SPLIT), pl.ds(OUT_SPLIT, D - OUT_SPLIT)
-        for d in (1, 3, 2):
-            at = rows_out.at[xh, c, xl, z, :, left]
-            a_first.append(go(at, at, along_x(d)))
-            at = rows_out.at[xh, c, xl, z, :, right]
-            b_first.append(go(at, at, along_z(d)))
-        cores = []
-        for o in outs:
-            cores.append(go(o.at[z, xh, c, mine], o.at[z, xh, c, mine], sibling))
-        at = rows_out.at[xh, c, xl, z]
-        cores.append(go(at, at, sibling))
-        for cp in a_first + b_first:
+        @pl.when(jnp.logical_not(away))
+        def _():
+            keep.wait()
+
+        g_out.start()
+        tok_own.wait()
+        norm_block(y)
+        g_proj.turn()
+        tok_ring.turn()
+        g_proj.pass_on()
+        g_out.turn()
+        for cp in spot_copies:
             cp.wait_recv()
 
-        a_second, b_second = [], []
-        for d in (1, 3, 2):
-            for o, (cols, a) in zip(outs, SPLITS):
-                left, right = pl.ds(0, a), pl.ds(a, cols - a)
-                at = o.at[z, :, c, :, left]
-                a_second.append(go(at, at, along_z(d)))
-                at = o.at[:, xh, c, mine, right]
-                b_second.append(go(at, at, along_x(d)))
-            left, right = pl.ds(0, OUT_SPLIT), pl.ds(OUT_SPLIT, D - OUT_SPLIT)
-            at = rows_out.at[:, c, :, z, :, left]
-            a_second.append(go(at, at, along_z(d)))
-            at = rows_out.at[xh, c, xl, :, :, right]
-            b_second.append(go(at, at, along_x(d)))
-
-        for d in (1, 3, 2):
-            fx, fxl, _, _, _ = along_x(4 - d)(xh, xl, y, z, c)
-            fz = (z + 4 - d) % 4
-            theirs = pl.ds(fxl * 64, 64)
-            for o, (cols, a) in zip(outs, SPLITS):
-                left, right = pl.ds(0, a), pl.ds(a, cols - a)
-                at = o.at[z, fx, c, theirs, left]
-                cores.append(go(at, at, sibling))
-                at = o.at[fz, xh, c, mine, right]
-                cores.append(go(at, at, sibling))
-            left, right = pl.ds(0, OUT_SPLIT), pl.ds(OUT_SPLIT, D - OUT_SPLIT)
-            at = rows_out.at[fx, c, fxl, z, :, left]
-            cores.append(go(at, at, sibling))
-            at = rows_out.at[xh, c, xl, fz, :, right]
-            cores.append(go(at, at, sibling))
-
-        at_a, at_b = iter(a_second), iter(b_second)
-        for d in (1, 3, 2):
-            fx, fxl, _, _, _ = along_x(4 - d)(xh, xl, y, z, c)
-            fz = (z + 4 - d) % 4
-            theirs = pl.ds(fxl * 64, 64)
-            for o, (cols, a) in zip(outs, SPLITS):
-                left, right = pl.ds(0, a), pl.ds(a, cols - a)
-                next(at_a).wait_recv()
-                at = o.at[fz, :, c, :, left]
-                cores.append(go(at, at, sibling))
-                next(at_b).wait_recv()
-                at = o.at[:, fx, c, theirs, right]
-                cores.append(go(at, at, sibling))
-            left, right = pl.ds(0, OUT_SPLIT), pl.ds(OUT_SPLIT, D - OUT_SPLIT)
-            next(at_a).wait_recv()
-            at = rows_out.at[:, c, :, fz, :, left]
-            cores.append(go(at, at, sibling))
-            next(at_b).wait_recv()
-            at = rows_out.at[fx, c, fxl, :, :, right]
-            cores.append(go(at, at, sibling))
-        for cp in cores:
+        cos, sin = [], []
+        freq, sign = freq_ref[0:1, :], freq_ref[1:2, :]
+        spot_cols = []
+        for k in range(4):
+            col = jnp.transpose(jnp.broadcast_to(spot_all[k, 0:1, :], (128, 128)))
+            spot_out[k] = col
+            spot_cols.append(col)
+            cos.append(jnp.cos(col * freq))
+            sin.append(jnp.sin(col * freq) * sign)
+        cos, sin = jnp.concatenate(cos, 0), jnp.concatenate(sin, 0)
+        low_half = xl == 0
+        reach = jnp.where(low_half, -1.0, 2048.0)
+        for k in range(4):
+            for j in range(8):
+                row = lax.broadcasted_iota(jnp.int32, (128, 128), 0) + k * 128
+                col = lax.broadcasted_iota(jnp.int32, (128, 128), 1) + j * 128
+                apart = (row - col + 512).astype(F32)
+                seen = apart <= spot_cols[k]
+                if j < 4:
+                    seen = seen & (apart <= reach)
+                else:
+                    seen = seen & (col - 512 <= row)
+                bias[pl.ds(k * 128, 128), pl.ds(j * 128, 128)] = jnp.where(seen, 0.0, NEG_FILL)
+
+        g_proj.near()
+        stay[1].wait()
+        stay[2].wait()
+        for cp in to_y[1] + to_y[2]:
             cp.wait_recv()
-        for cp in started:
+        g_gu.start()
+        g_down.start()
+        g_proj.far()
+        g_out.pass_on()
+        tok_ring.near()
+        norm_block((y + 3) % 4)
+        norm_block((y + 1) % 4)
+        g_proj.finish()
+        wp_load = near(gp, wp_v)
+        wp_load.start()
+        g_out.near()
+        tok_ring.far()
+        cot_ring.start()
+        norm_block((y + 2) % 4)
+        normed_save = near(normed, normed_out)
+        normed_save.start()
+
+        wp_load.wait()
+        left = normed[...].reshape(count, D)
+        lane = lax.broadcasted_iota(jnp.int32, (count, 128), 1)
+        upper = lane >= 64
+        raw = dot(left, wp_v[:, :, :, :, pl.ds(Q_COLS, 128)].reshape(D, 128))
+        turned = raw * jnp.where(upper, 1.0, cos) + swap_halves(raw) * jnp.where(upper, 0.0, sin)
+        kv[1] = turned.astype(BF16)
+        kv_copy.start()
+        g_out.far()
+        g_gu.turn()
+        g_down.turn()
+        for j in range(2):
+            raw2 = dot(left, wp_v[:, :, :, :, pl.ds(j * 256, 256)].reshape(D, 256))
+            for e in range(2):
+                raw = raw2[:, e * 128 : e * 128 + 128]
+                turned = (raw * cos + swap_halves(raw) * sin).astype(BF16).astype(F32) * (HEAD_DIM ** (-0.5))
+                pair = j * 2 + e
+                q_s[2 * pair] = jnp.where(upper, 0.0, turned).astype(BF16)
+                q_s[2 * pair + 1] = jnp.where(upper, 0.0, pltpu.roll(turned, 64, 1)).astype(BF16)
+        kv_copy.wait_recv()
+        for k in range(2):
+            vx[k] = jnp.where(upper, kv[k].astype(F32), 1.0).astype(BF16)
+        q_save = near(q_s, q_out)
+        q_save.start()
+        kv_save = near(kv, kv_out)
+        kv_save.start()
+        g_out.finish()
+        wo_load = near(go, wo_v)
+        wo_load.start()
+        cot_ring.turn()
+
+        def attend(pair):
+            for b in range(2):
+                rs = pl.ds(b * 256, 256)
+                seen = 256 * (b + 1)
+                lane = lax.broadcasted_iota(jnp.int32, (256, 128), 1) < 64
+                found = []
+                for e in range(2):
+                    q = q_s[2 * pair + e, rs]
+                    s0 = dot(q, kv[0], NT) + bias[rs, pl.ds(0, 512)]
+                    s1 = dot(q, kv[1, pl.ds(0, seen)], NT) + bias[rs, pl.ds(512, seen)]
+                    m = jnp.maximum(jnp.max(s0, -1, keepdims=True), jnp.max(s1, -1, keepdims=True))
+                    p0 = jnp.exp(s0 - m).astype(BF16)
+                    p1 = jnp.exp(s1 - m).astype(BF16)
+                    o = dot(p0, vx[0]) + dot(p1, vx[1, pl.ds(0, seen)])
+                    r = pltpu.roll(o, 64, 1)
+                    found.append((o, r))
+                    log_total = m + jnp.log(jnp.where(lane, o, r))
+                    lse_out[2 * pair + e, :, rs] = jnp.transpose(log_total)[0:8]
+                (o, r), (o2, r2) = found
+                both = jnp.where(lane, r / o, o2 / r2)
+                att[rs, pl.ds(pl.multiple_of(pair * 128, 128), 128)] = both.astype(BF16)
+
+        def two_pairs(k):
+            def body(i, _):
+                attend(2 * k + i)
+                return 0
+
+            lax.fori_loop(0, 2, body, 0)
+
+        two_pairs(0)
+        g_gu.pass_on()
+        g_down.pass_on()
+        two_pairs(1)
+        att_save = near(att, att_out)
+        att_save.start()
+        wo_load.wait()
+
+        for j in range(4):
+            cols = pl.ds(j * 512, 512)
+            w = wo_v[:, :, :, :, :, cols].reshape(Q_COLS, 512)
+            part[:, :, cols] = dot(att[...], w).astype(BF16).reshape(4, rows, 512)
+        branch.start()
+        g_gu.near()
+        g_down.near()
+        branch.turn()
+        cot_ring.near()
+        cot_ring.far()
+        branch.finish()
+
+        def mid(r, _):
+            rs = pl.ds(r * 32, 32)
+            v = tok_ref[rs].astype(F32) + branch.rows(rs)
+            middle_out[rs] = v
+            inv = lax.rsqrt(jnp.mean(v * v, -1, keepdims=True) + EPS)
+            own_two[rs] = (v * inv).astype(BF16)
+            return 0
+
+        lax.fori_loop(0, rows // 32, mid, 0)
+        two_own = near(own_two, two_all.at[y])
+        two_own.start()
+        two_ring.start()
+        g_gu.far()
+        g_down.far()
+        two_ring.turn()
+        two_ring.near()
+        two_ring.far()
+        g_gu.finish()
+        g_down.finish()
+        for cp in (cot_own, normed_save, q_save, kv_save, att_save, two_own):
+            cp.wait()
+        for group in to_y:
+            for cp in group:
+                cp.wait_send()
+        for cp in spot_copies + [kv_copy]:
             cp.wait_send()
-
-    outs = [struct((4, 2, 2, 128, b.shape[2])) for b in blocks] + [struct((2, 2, 2, 4, 16, D))]
-    copies = 3 * n + 1 + 7 * 3 * (n + 1) * 2
-    got = comm_call(kernel, "gather_weights", ident, [*blocks, out_rows], outs, copies, n + 1)
-    return [g.reshape(D, g.shape[-1]) for g in got[:-1]] + [got[-1].reshape(Q_COLS, D)]
+        for thing in (g_proj, g_out, g_gu, g_down, tok_ring, cot_ring, two_ring, branch):
+            thing.sent()
+
+    anywhere, vmem = pl.BlockSpec(memory_space=pl.ANY), pl.BlockSpec(memory_space=pltpu.VMEM)
+    outs = [
+        (struct((4, rows, D)), anywhere),
+        (struct((4, rows, D)), anywhere),
+        (struct((4, 2, 2, 128, PROJ)), anywhere),
+        (struct((4, 2, 2, 128, 2 * HID)), anywhere),
+        (struct((4, 2, 2, 128, HID)), anywhere),
+        (struct((2, 2, 2, 4, 16, D)), anywhere),
+        (struct((REPEAT, count, 128)), anywhere),
+        (struct((2, count, 128)), anywhere),
+        (struct((count, Q_COLS)), anywhere),
+        (struct((REPEAT, 8, count), F32), vmem),
+        (struct((4, 128, 128), F32), vmem),
+        (struct((rows, D), F32), vmem),
+        (struct((4, rows, D)), anywhere),
+    ]
+    copies = 9 + 1 + 3 + 6 * 3 + 6 + 1 + 31 * 4
+    return pl.pallas_call(
+        kernel,
+        out_shape=[o[0] for o in outs],
+        in_specs=[vmem] * 8,
+        out_specs=[o[1] for o in outs],
+        scratch_shapes=[
+            pltpu.VMEM((4, rows, D), BF16),
+            pltpu.VMEM((4, rows, D), BF16),
+            pltpu.VMEM((4, 2, 2, 128, PROJ), BF16),
+            pltpu.VMEM((2, 2, 2, 4, 16, D), BF16),
+            pltpu.VMEM((REPEAT, count, 128), BF16),
+            pltpu.VMEM((2, count, 128), BF16),
+            pltpu.VMEM((2, count, 128), BF16),
+            pltpu.VMEM((count, 2 * count), F32),
+            pltpu.VMEM((count, Q_COLS), BF16),
+            pltpu.VMEM((4, rows, D), BF16),
+            pltpu.VMEM((2, rows, D // 2), BF16),
+            pltpu.VMEM((2, rows, D), BF16),
+            pltpu.VMEM((4, 8, 128), F32),
+            pltpu.VMEM((rows, D), BF16),
+            pltpu.SemaphoreType.DMA((copies,)),
+            pltpu.SemaphoreType.DMA((copies,)),
+            pltpu.SemaphoreType.DMA((16,)),
+        ],
+        name="forward_attention",
+        compiler_params=pltpu.CompilerParams(
+            collective_id=ident, has_side_effects=True, vmem_limit_bytes=VMEM_LIMIT
+        ),
+    )(tokens, cotangent, spots, freqs, w_proj, w_gu, w_down, out_rows)
+
+
+def swap(part, to, ident, name):
+    def kernel(src, dst, send, recv, local):
+        greet([to], False)
+        cp = Copies(send, recv)(src, dst, to)
+        cp.start()
+        cp.wait()
+
+    (out,) = comm_call(kernel, name, ident, [part], [struct(part.shape, part.dtype)], 1)
+    return out
 
 
 def across(parts, rows_part, ident, name, stage):
@@ -487,11 +871,6 @@
     return lax.dot_general(left, right, (dims, ((), ())), preferred_element_type=F32).astype(out)
 
 
-NN = ((1,), (0,))
-NT = ((1,), (1,))
-TN = ((0,), (0,))
-
-
 def shards(tokens, positions, attn_in, attn_out, attn_gain, mlp_in, mlp_down, mlp_gain, cotangent):
     xh, xl, y, z, c = place()
     rows = tokens.shape[0]
@@ -511,51 +890,36 @@
     w_gu = jnp.concatenate([by_y(mlp_f[:, :FF]), by_y(mlp_f[:, FF:])], -1)
     w_gu = (w_gu * gain_two[:, :, None]).astype(BF16).transpose(1, 0, 2)
     w_down = by_y(mlp_down).transpose(1, 0, 2)
-    proj_w, gu_w, down_w, out_w = gather_weights([w_proj, w_gu, w_down], attn_out, 0)
-
-    spots = jnp.broadcast_to(positions[None, :], (8, rows))
-    tokens_all, cot_all, spots_all = ring_gather([tokens, cotangent, spots], 1, "gather_tokens")
-    seq_tokens = tokens_all.reshape(count, D).astype(F32)
-    seq_cot = cot_all.reshape(count, D)
-    seq_pos = spots_all[:, 0].reshape(count)
-
-    normed_one_all = (seq_tokens * inv_norm(seq_tokens)).astype(BF16)
-    projected = mm(normed_one_all, proj_w, NN)
+    spots = jnp.broadcast_to(positions.astype(F32)[None, :], (8, rows))
+    lanes = jnp.arange(128)
+    inv_freq = ROPE_BASE ** (-2.0 * (lanes % 32).astype(F32) / HEAD_DIM)
+    signs = jnp.where(lanes % 64 < 32, -1.0, 1.0)
+    freqs = jnp.zeros((8, 128), F32).at[0].set(inv_freq).at[1].set(signs)
+    (normed_one_all, cot_all, proj_w, gu_w, down_w, out_w, q_all, kv_all, attended_low, lse, spots_all, middle, seq_two) = (
+        forward_attention(tokens, cotangent, spots, freqs, w_proj, w_gu, w_down, attn_out, 0)
+    )
+    normed_one_all = normed_one_all.reshape(count, D)
+    seq_cot, seq_two = cot_all.reshape(count, D), seq_two.reshape(count, D)
+    proj_w, gu_w, down_w = (w.reshape(D, w.shape[-1]) for w in (proj_w, gu_w, down_w))
+    out_w = out_w.reshape(Q_COLS, D)
+    seq_pos = spots_all.reshape(count, 128)[:, 0]
     cosines, sines = angles(seq_pos)
-    queries = rotary(projected[:, :Q_COLS].reshape(count, REPEAT, HEAD_DIM), cosines, sines).astype(BF16)
-    keys = rotary(projected[:, None, Q_COLS : Q_COLS + HEAD_DIM], cosines, sines)[:, 0].astype(BF16)
-    keys_values = jnp.concatenate([keys, projected[:, Q_COLS + HEAD_DIM :].astype(BF16)], -1)
-    theirs = swap(keys_values, half_partner, 2, "swap_keys")
-    low_half = xl == 0
-    kv_all = jnp.concatenate(
-        [jnp.where(low_half, keys_values, theirs), jnp.where(low_half, theirs, keys_values)], 0
-    )
+    queries = q_all[:, :, :HEAD_DIM].transpose(1, 0, 2)
+    kv_all = kv_all.reshape(2 * count, 2 * HEAD_DIM)
     keys_all, values_all = kv_all[:, :HEAD_DIM], kv_all[:, HEAD_DIM:]
-    query_index = xl * count + jnp.arange(count, dtype=jnp.int32)
-    key_index = jnp.arange(2 * count, dtype=jnp.int32)
-    visible = (key_index[None, :] <= query_index[:, None]) & (
-        query_index[:, None] - key_index[None, :] <= seq_pos[:, None]
-    )
+    row = jnp.arange(count, dtype=jnp.int32)[:, None]
+    col = jnp.arange(2 * count, dtype=jnp.int32)[None, :]
+    apart = row + count - col
+    visible = (apart.astype(F32) <= seq_pos[:, None]) & jnp.where(col < count, xl == 1, apart >= 0)
+    log_total = lse[:, 0, :, None]
 
     def masked_scores():
         raw = jnp.einsum("qhd,kd->hqk", queries, keys_all, preferred_element_type=F32)
-        return jnp.where(visible[None], raw * scale, NEG_FILL)
-
-    scores = masked_scores()
-    peak = jnp.max(scores, -1, keepdims=True)
-    exps = jnp.exp(scores - peak)
-    row_total = jnp.sum(exps, -1, keepdims=True)
-    probs_low = (exps / row_total).astype(BF16)
-    log_total = peak + jnp.log(row_total)
-    attended = jnp.einsum("hqk,kd->qhd", probs_low, values_all, preferred_element_type=F32)
-    attended_low = attended.reshape(count, Q_COLS).astype(BF16)
-    branch = ring_sum(mm(attended_low, out_w, NN, BF16), 3, "sum_branch")
+        return jnp.where(visible[None], raw, NEG_FILL)
+
     inputs = tokens.astype(F32)
-    middle = inputs + branch
     inv_two = inv_norm(middle)
     normed_two = middle * inv_two
-    (seq_two,) = ring_gather([normed_two.astype(BF16)], 4, "gather_two")
-    seq_two = seq_two.reshape(count, D)
 
     gate_up = mm(seq_two, gu_w, NN)
     gate, up = gate_up[:, :HID], gate_up[:, HID:]
@@ -572,19 +936,18 @@
     term_gu = mm(seq_two, grad_gu, TN, BF16)
     term_down = mm(seq_cot, hidden_act, TN, BF16)
 
-    (seq_branch,) = ring_gather([grad_middle.astype(BF16)], 7, "gather_branch")
-    seq_branch = seq_branch.reshape(count, D)
+    seq_branch = ring_gather(grad_middle.astype(BF16), 7, "gather_branch").reshape(count, D)
     grad_att = mm(seq_branch, out_w, NT, BF16).reshape(count, REPEAT, HEAD_DIM)
     probs = jnp.exp(masked_scores() - log_total)
     grad_probs = jnp.einsum("qhd,kd->hqk", grad_att, values_all, preferred_element_type=F32)
     row_delta = jnp.sum(probs * grad_probs, -1, keepdims=True)
     grad_scores = (probs * (grad_probs - row_delta)).astype(BF16)
     grad_q = jnp.einsum("hqk,kd->qhd", grad_scores, keys_all, preferred_element_type=F32) * scale
-    grad_k = jnp.einsum("hqk,qhd->kd", grad_scores, queries, preferred_element_type=F32) * scale
+    grad_k = jnp.einsum("hqk,qhd->kd", grad_scores, queries, preferred_element_type=F32)
     grad_v = jnp.einsum("hqk,qhd->kd", probs.astype(BF16), grad_att, preferred_element_type=F32)
     grad_kv = jnp.concatenate([grad_k, grad_v], -1).reshape(2, count, 2 * HEAD_DIM)
-    away = lax.dynamic_index_in_dim(grad_kv, 1 - xl, 0, False).astype(BF16)
-    grad_kv = lax.dynamic_index_in_dim(grad_kv, xl, 0, False)
+    away = grad_kv[0].astype(BF16)
+    grad_kv = grad_kv[1]
     grad_kv = grad_kv + swap(away, half_partner, 8, "swap_grad_keys").astype(F32)
     grad_q = rotary(grad_q, cosines, -sines).reshape(count, Q_COLS)
     grad_k = rotary(grad_kv[:, None, :HEAD_DIM], cosines, -sines)[:, 0]

time: 659 us -> 486 us (0.74)
  Pallas kernels: 426 us -> 306 us
  other arithmetic: 91.6 us -> 65.9 us
  matrix products: 107 us -> 84.3 us
  local copies, waits for them, and re-layouts: 25.6 us -> 18.6 us
    pallas_call x14 -> x5, Pallas kernels: 426 us -> 122 us  [comm_call(): pl.pallas_call(kernel, out_shape=outs, in_specs=[pl.BlockSpec(memory_spac...]
    pallas_call x0 -> x5, Pallas kernels: none -> 184 us  [the longest x1 111 us: forward_attention(): pl.pallas_call(kernel, out_shape=[o[0] for o in outs], in_specs=[vmem] *...]
    reduce_sum x5 -> x0, other arithmetic: 16.6 us -> none  [the longest x4 8.55 us: ring_sum(): return own.astype(F32) + jnp.sum(others.astype(F32), 0)]
    dot_general x1 -> x0, matrix products: 7.87 us -> none  [shards(): jnp.einsum('hqk,kd->qhd', probs_low, values_all, preferred_element_type=F32)]
    dot_general x12 -> x10, matrix products: 67.6 us -> 62.6 us  [mm(): lax.dot_general(left, right, (dims, ((), ())), preferred_element_type=F32)]
where the time goes in v2:
time: 486 us; the launch traced here: 477 us
  Pallas kernels  306 us (63%)
  matrix products  84.3 us (17%)
  other arithmetic  65.9 us (14%)
  local copies, waits for them, and re-layouts  18.6 us (4%)
    pallas_call x5, Pallas kernels, comm_call(): pl.pallas_call(kernel, out_shape=outs, in_specs=[pl.BlockSpec(memory_spac...  122 us
    pallas_call x1, Pallas kernels, forward_attention(): pl.pallas_call(kernel, out_shape=[o[0] for o in outs], in_specs=[vmem] *...  111 us
    dot_general x10, matrix products, mm(): lax.dot_general(left, right, (dims, ((), ())), preferred_element_type=F32)  62.6 us
    pallas_call x3, Pallas kernels, ring_sum(): pl.pallas_call(kernel, out_shape=struct((rows, cols), F32), in_specs=[pl....  56.2 us
    convert_element_type x20, other arithmetic, total(): return (own.astype(F32) + jnp.sum(others.astype(F32), 0)).astype(BF16)  25.2 us
    pallas_call x1, Pallas kernels, ring_gather(): pl.pallas_call(kernel, out_shape=struct((4,) + part.shape, part.dtype), i...  16.5 us

profile of v2, /device:TPU:0, one launch (start us, length us, event | category | flops | bytes accessed | tf_op | source)
XLA Modules:
  0.0 476.9 jit_solution(16879277880627737135)
XLA Ops:
  5.6 111.3 %forward_attention.1 = (bf16[4,128,2048]{2,1,0:T(8,128)(2,1)}, bf16[4,128,2048]{2,1,0:T(8,128)(2,1)}, bf16[4,2,2,128,640]{4,3,2,1,0:T(8,128)(2,1)}, bf16[4,2,2,1...) custom-call(bf16[128,2048]{1,0:T(8,128)(2,1)} %tok_ref.1, ...), custom_call_target="tpu_custom_call" | custom-call | tf_op jit(solution)/shard_map/forward_attention/pallas_call | solution.py:673
  116.9 10.5 %fusion.71 = f32[512,2816]{1,0:T(8,128)S(1)} fusion(bf16[512,2048]{1,0:T(8,128)(2,1)} %bitcast.253, bf16[2048,2816]{1,0:T(8,128)(2,1)} %bitcast.244), kind=kOutput, calls=%fused_computation.196 | convolution fusion | flops 5905580032 | bytes 19398656 | tf_op jit(solution)/shard_map/dot_general | solution.py:871
  127.4 5.7 %multiply_convert_fusion.1 = (bf16[512,1408]{1,0:T(8,128)(2,1)S(1)}, bf16[512,1408]{1,0:T(8,128)(2,1)}, bf16[512,1408]{1,0:T(8,128)(2,1)}) fusion(f32[512,2816]{1,0:T(8,128)S(1)} %fusion.71, bf16[512,2048]{1,0:T(8,128)(2,1)S(1)} %bitcast.251, bf16[2048,1408]{1,0:T(8,128)(2,1)S(1)} %bitcast.249), kind=kOutput, calls=%fused_computation.26 | convolution fusion | flops 2963603456 | bytes 17956864 | tf_op jit(solution)/shard_map/dot_general | solution.py:871
  134.3 8.5 %convolution_convert_fusion.4 = bf16[512,2048]{1,0:T(8,128)(2,1)} fusion(bf16[2048,2816]{1,0:T(8,128)(2,1)S(1)} %bitcast.247, bf16[512,1408]{1,0:T(8,128)(2,1)} %get-tuple-element.107, bf16[512,1408]{1,0:T(8,128)(2,1)S(1)} %get-tuple-element.106), kind=kOutput, calls=%fused_computation.21 | convolution fusion | flops 5912395776 | bytes 16515072 | tf_op jit(solution)/shard_map/dot_general | solution.py:871
  142.7 18.4 %sum_grad_two.1 = f32[128,2048]{1,0:T(8,128)} custom-call(bf16[4,128,2048]{2,1,0:T(8,128)(2,1)} %bitcast.210), custom_call_target="tpu_custom_call" | custom-call | tf_op jit(solution)/shard_map/sum_grad_two/pallas_call | solution.py:248
  164.1 16.5 %gather_branch.1 = bf16[4,128,2048]{2,1,0:T(8,128)(2,1)} custom-call(bf16[128,2048]{1,0:T(8,128)(2,1)} %fusion.67.src), custom_call_target="tpu_custom_call" | custom-call | tf_op jit(solution)/shard_map/gather_branch/pallas_call | solution.py:282
  180.7 3.6 convolution_convert_fusion.7
  185.2 2.3 fusion.29
  188.5 8.8 %fusion = (f32[8,512]{1,0:T(8,128)S(1)}, f32[1024,512,8]{1,0,2:T(8,128)}) fusion(f32[1024,512,8]{1,0,2:T(8,128)S(1)} %fusion.29, f32[8,512]{1,0:T(8,128)S(1)} %bitcast.237, pred[512,1024]{0,1:T(8,128)(4,1)S(1)} %fusion.16, bf16[512,8,64]{0,2,1:T(8,128)(2,1)S(1)} %bitcast.222, bf16[1024,128]{1,0:T(8,128)(2,1)S(1)} %bitcast.204), kind=kOutput, calls=%fused_computation.2 | convolution fusion | flops 553644032 | bytes 34897920 | tf_op jit(solution)/shard_map/qhd,kd->hqk/dot_general | solution.py:942
  197.3 8.2 %fusion.2 = bf16[8,512,1024]{1,2,0:T(8,128)(2,1)S(1)} fusion(f32[1024,512,8]{1,0,2:T(8,128)} %get-tuple-element.130, f32[1024,512,8]{1,0,2:T(8,128)S(1)} %fusion.29, f32[8,512]{1,0:T(8,128)S(1)} %get-tuple-element.129, f32[8,512]{1,0:T(8,128)S(1)} %bitcast.238, pred[512,1024]{0,1:T(8,128)(4,1)S(1)} %fusion.16), kind=kLoop, calls=%fused_computation.4 | loop fusion | flops 20971520 | bytes 42500096 | tf_op jit(solution)/shard_map/convert_element_type | solution.py:944
  210.1 3.2 fusion.20
  213.3 5.7 %convolution_bitcast_fusion = f32[1024,64]{1,0:T(8,128)S(1)} fusion(bf16[8,512,1024]{1,2,0:T(8,128)(2,1)} %copy-done, bf16[8,512,128]{2,1,0:T(8,128)(2,1)S(1)} %copy-done.11), kind=kOutput, calls=%fused_computation.52 | convolution fusion | flops 536870912 | bytes 9699328 | tf_op jit(solution)/shard_map/hqk,qhd->kd/dot_general | solution.py:946
  219.8 5.3 %swap_grad_keys.1 = bf16[512,128]{1,0:T(8,128)(2,1)} custom-call(bf16[512,128]{1,0:T(8,128)(2,1)} %fusion.48.src), custom_call_target="tpu_custom_call" | custom-call | tf_op jit(solution)/shard_map/swap_grad_keys/pallas_call | solution.py:117
  226.2 1.6 fusion.40
  228.3 5.1 %convolution_convert_fusion.2 = bf16[2048,640]{1,0:T(8,128)(2,1)} fusion(bf16[512,2048]{1,0:T(8,128)(2,1)} %bitcast.255, bf16[512,64]{0,1:T(8,128)(2,1)S(1)} %copy.78, bf16[512,64]{0,1:T(8,128)(2,1)S(1)} %copy.77, bf16[512,512]{0,1:T(8,128)(2,1)S(1)} %bitcast.224), kind=kOutput, calls=%fused_computation.19 | convolution fusion | flops 1345454080 | bytes 5373952 | tf_op jit(solution)/shard_map/dot_general | solution.py:871
  233.4 2.6 convolution_convert_fusion.3
  236.2 9.0 %convolution_convert_fusion = bf16[2048,2816]{1,0:T(8,128)(2,1)} fusion(bf16[512,2048]{1,0:T(8,128)(2,1)S(1)} %bitcast.254, bf16[512,1408]{1,0:T(8,128)(2,1)S(1)} %copy-done.54, bf16[512,1408]{1,0:T(8,128)(2,1)S(1)} %copy-done.53), kind=kOutput, calls=%fused_computation.10 | convolution fusion | flops 5917114368 | bytes 16515072 | tf_op jit(solution)/shard_map/dot_general | solution.py:871
  245.2 5.5 %convolution_convert_fusion.1 = bf16[2048,1408]{1,0:T(8,128)(2,1)} fusion(bf16[512,2048]{1,0:T(8,128)(2,1)S(1)} %bitcast.252, bf16[512,1408]{1,0:T(8,128)(2,1)S(1)} %copy-done.50), kind=kOutput, calls=%fused_computation.14 | convolution fusion | flops 2955673600 | bytes 9306112 | tf_op jit(solution)/shard_map/dot_general | solution.py:871
  250.7 17.8 %grads_core.1 = (bf16[4,2,128,640]{3,2,1,0:T(8,128)(2,1)}, bf16[4,2,128,2816]{3,2,1,0:T(8,128)(2,1)}, bf16[4,2,128,1408]{3,2,1,0:T(8,128)(2,1)}, bf16[2,2,4,16,2048]{4,3,2,1,0:T(8,128)(2,1)}) custom-call(bf16[4,2,2,128,640]{4,3,2,1,0:T(8,128)(2,1)} %bitcast.199, bf16[4,2,2,128,2816]{4,3,2,1,0:T(8,128)(2,1)} %bitcast.195, ...), custom_call_target="tpu_custom_call" | custom-call | tf_op jit(solution)/shard_map/grads_core/pallas_call | solution.py:117
  268.6 3.1 fusion.13.refs_3_
  271.7 4.2 fusion.10.refs_2_
  275.8 8.4 %fusion.5.refs_1_ = bf16[4,2,128,2816]{3,2,1,0:T(8,128)(2,1)} fusion(bf16[4,2,128,2816]{3,2,1,0:T(8,128)(2,1)} %get-tuple-element.83, bf16[4,2,2,128,2816]{4,3,2,1,0:T(8,128)(2,1)} %bitcast.196, s32[]{:T(128)S(6)} %select_n.136), kind=kLoop, calls=%fused_computation.9 | loop fusion | flops 11534336 | bytes 17301508 | tf_op jit(solution)/shard_map/convert_element_type | solution.py:817
  285.7 66.5 %grads_first.1 = (bf16[3,2,128,384]{3,2,1,0:T(8,128)(2,1)}, bf16[3,4,64,256]{3,2,1,0:T(8,128)(2,1)}, bf16[3,2,128,1408]{3,2,1,0:T(8,128)(2,1)}, bf16[3,4,64,1408...) custom-call(bf16[4,2,128,640]{3,2,1,0:T(8,128)(2,1)} %fusion.12.refs, ...), custom_call_target="tpu_custom_call" | custom-call | tf_op jit(solution)/shard_map/grads_first/pallas_call | solution.py:117
  355.9 1.6 convert_reduce_fusion.2
  367.9 19.0 %grads_second.1 = (bf16[3,64,384]{2,1,0:T(8,128)(2,1)}, bf16[3,64,256]{2,1,0:T(8,128)(2,1)}, bf16[3,64,1408]{2,1,0:T(8,128)(2,1)}, bf16[3,64,1408]{2,1,0:T(8,128...) custom-call(bf16[2,128,384]{2,1,0:T(8,128)(2,1)} %add_convert_fusion, ...), custom_call_target="tpu_custom_call" | custom-call | tf_op jit(solution)/shard_map/grads_second/pallas_call | solution.py:117
  401.0 13.3 %grads_y.1 = (bf16[4,16,640]{2,1,0:T(8,128)(2,1)}, bf16[4,16,2816]{2,1,0:T(8,128)(2,1)}, bf16[4,16,1408]{2,1,0:T(8,128)(2,1)}, bf16[16,2048]{1,0:T(8,128)(2,1)}) custom-call(bf16[4,16,640]{2,1,0:T(8,128)(2,1)} %pad_maximum_fusion.10.refs_0_, bf16[4,16,2816]{2,1,0:T(8,128)(2,1)} %pad_maximum_fusion.5.refs_1_, bf16[4,16,1408]{2,1,0:T(8,128)(2,1)} %pad_maximum_fusion.9.refs_2_, ...), custom_call_target="tpu_custom_call" | custom-call | tf_op jit(solution)/shard_map/grads_y/pallas_call | solution.py:117
  417.5 2.0 multiply_reduce_fusion.3
  421.9 4.9 %convolution_convert_fusion.5 = bf16[512,2048]{1,0:T(8,128)(2,1)} fusion(bf16[2048,640]{1,0:T(8,128)(2,1)} %bitcast.250, bf16[512,64]{0,1:T(8,128)(2,1)S(1)} %copy-done.32, bf16[512,64]{0,1:T(8,128)(2,1)S(1)} %copy.77, bf16[512,512]{0,1:T(8,128)(2,1)S(1)} %bitcast.225), kind=kOutput, calls=%fused_computation.22 | convolution fusion | flops 1345191936 | bytes 5373952 | tf_op jit(solution)/shard_map/dot_general | solution.py:871
  426.8 20.3 %sum_grad_one.1 = f32[128,2048]{1,0:T(8,128)} custom-call(bf16[4,128,2048]{2,1,0:T(8,128)(2,1)} %bitcast.208), custom_call_target="tpu_custom_call" | custom-call | tf_op jit(solution)/shard_map/sum_grad_one/pallas_call | solution.py:248
  448.8 7.3 %convolution_convert_fusion.6 = bf16[512,2048]{1,0:T(8,128)(2,1)} fusion(bf16[512,1408]{1,0:T(8,128)(2,1)S(1)} %copy-done.51, bf16[2048,1408]{1,0:T(8,128)(2,1)} %bitcast.248), kind=kOutput, calls=%fused_computation.23 | convolution fusion | flops 2953838592 | bytes 9306112 | tf_op jit(solution)/shard_map/dot_general | solution.py:871
  456.2 17.5 %sum_outputs.1 = f32[128,2048]{1,0:T(8,128)} custom-call(bf16[4,128,2048]{2,1,0:T(8,128)(2,1)} %bitcast.209), custom_call_target="tpu_custom_call" | custom-call | tf_op jit(solution)/shard_map/sum_outputs/pallas_call | solution.py:248
  473.7 2.9 fusion.26
  (239 shorter events, 54.1 us)
Async XLA Ops:
  3.5 123.9 %copy-start.37 = (f32[16]{0:T(128)}, f32[16]{0:T(128)S(1)}, u32[]{:S(2)}) copy-start(f32[16]{0:T(128)S(1)} %convert_element_type.328) | copy-start | bytes 196
  116.9 10.5 %copy-start.42 = (bf16[4,2,2,128,1408]{4,3,2,1,0:T(8,128)(2,1)S(1)}, bf16[4,2,2,128,1408]{4,3,2,1,0:T(8,128)(2,1)}, u32[]{:S(2)}) copy-start(bf16[4,2,2,128,1408]{4,3,2,1,0:T(8,128)(2,1)} %get-tuple-element.72) | copy-start | bytes 17301508
  116.9 10.5 %copy-start.43 = (bf16[4,128,2048]{2,1,0:T(8,128)(2,1)S(1)}, bf16[4,128,2048]{2,1,0:T(8,128)(2,1)}, u32[]{:S(2)}) copy-start(bf16[4,128,2048]{2,1,0:T(8,128)(2,1)} %get-tuple-element.73) | copy-start | bytes 6291460
  116.9 17.4 %slice-start.2 = ((s8[11534336]{0:T(1024)(128)(4,1)}), s8[4194304]{0:T(1024)(128)(4,1)S(1)}, s32[]{:S(2)}) async-start(s8[11534336]{0:T(1024)(128)(4,1)} %bitcast.245), calls=%async_computation.2 | async-start | bytes 8388608
  116.9 17.4 %slice-start.3 = ((s8[11534336]{0:T(1024)(128)(4,1)}), s8[4194304]{0:T(1024)(128)(4,1)S(1)}, s32[]{:S(2)}) async-start(s8[11534336]{0:T(1024)(128)(4,1)} %bitcast.245), calls=%async_computation.3 | async-start | bytes 8388608
  127.4 6.9 %slice-start.4 = ((s8[11534336]{0:T(1024)(128)(4,1)}), s8[3145728]{0:T(1024)(128)(4,1)S(1)}, s32[]{:S(2)}) async-start(s8[11534336]{0:T(1024)(128)(4,1)} %bitcast.245), calls=%async_computation.4 | async-start | bytes 6291456
  142.7 18.5 %copy-start.2 = (f32[128,2048]{1,0:T(8,128)S(1)}, f32[128,2048]{1,0:T(8,128)}, u32[]{:S(2)}) copy-start(f32[128,2048]{1,0:T(8,128)} %get-tuple-element.69) | copy-start | bytes 3145732
  142.7 20.2 %copy-start.9 = (bf16[128,2048]{1,0:T(8,128)(2,1)S(1)}, bf16[128,2048]{1,0:T(8,128)(2,1)}, u32[]{:S(2)}) copy-start(bf16[128,2048]{1,0:T(8,128)(2,1)} %cot_ref.1) | copy-start | bytes 1572868
  161.4 19.3 %copy-start.35 = (f32[128]{0:T(128)}, f32[128]{0:T(128)S(1)}, u32[]{:S(2)}) copy-start(f32[128]{0:T(128)S(1)} %add_rsqrt_fusion.1) | copy-start | bytes 1540
  163.0 17.7 %copy-start.40 = (f32[128]{0:T(128)}, f32[128]{0:T(128)S(1)}, u32[]{:S(2)}) copy-start(f32[128]{0:T(128)S(1)} %broadcast_multiply_fusion.3) | copy-start | bytes 1540
  219.0 9.3 %copy-start.23 = (bf16[512,8,64]{0,2,1:T(8,128)(2,1)S(1)}, bf16[512,8,64]{0,2,1:T(8,128)(2,1)}, u32[]{:S(2)}) copy-start(bf16[512,8,64]{0,2,1:T(8,128)(2,1)} %pad_maximum_fusion.4) | copy-start | bytes 1572868
  228.3 5.1 %copy-start.31 = (bf16[512,64]{0,1:T(8,128)(2,1)}, bf16[512,64]{0,1:T(8,128)(2,1)S(1)}, u32[]{:S(2)}) copy-start(bf16[512,64]{0,1:T(8,128)(2,1)S(1)} %copy.78) | copy-start | bytes 196612
  228.3 5.1 %copy-start.16 = (bf16[4,128,2048]{2,1,0:T(8,128)(2,1)S(1)}, bf16[4,128,2048]{2,1,0:T(8,128)(2,1)}, u32[]{:S(2)}) copy-start(bf16[4,128,2048]{2,1,0:T(8,128)(2,1)} %gather_branch.1) | copy-start | bytes 6291460
  236.2 9.0 %copy-start.44 = (bf16[4,128,2048]{2,1,0:T(8,128)(2,1)S(1)}, bf16[4,128,2048]{2,1,0:T(8,128)(2,1)}, u32[]{:S(2)}) copy-start(bf16[4,128,2048]{2,1,0:T(8,128)(2,1)} %get-tuple-element.73) | copy-start | bytes 6291460
  236.2 9.0 %copy-start.50 = (bf16[512,1408]{1,0:T(8,128)(2,1)S(1)}, bf16[512,1408]{1,0:T(8,128)(2,1)}, u32[]{:S(2)}) copy-start(bf16[512,1408]{1,0:T(8,128)(2,1)} %get-tuple-element.108) | copy-start | bytes 4325380
  275.8 8.4 %copy-start.8 = (bf16[2048,640]{1,0:T(8,128)(2,1)S(1)}, bf16[2048,640]{1,0:T(8,128)(2,1)}, u32[]{:S(2)}) copy-start(bf16[2048,640]{1,0:T(8,128)(2,1)} %convolution_convert_fusion.2) | copy-start | bytes 7864324
  275.8 8.4 %copy-start.17 = (bf16[4,2,128,640]{3,2,1,0:T(8,128)(2,1)S(1)}, bf16[4,2,128,640]{3,2,1,0:T(8,128)(2,1)}, u32[]{:S(2)}) copy-start(bf16[4,2,128,640]{3,2,1,0:T(8,128)(2,1)} %get-tuple-element.82) | copy-start | bytes 3932164
  285.7 67.7 %copy-start.7 = (bf16[2,2,4,16,2048]{4,3,2,1,0:T(8,128)(2,1)S(1)}, bf16[2,2,4,16,2048]{4,3,2,1,0:T(8,128)(2,1)}, u32[]{:S(2)}) copy-start(bf16[2,2,4,16,2048]{4,3,2,1,0:T(8,128)(2,1)} %fusion.13.refs_3_) | copy-start | bytes 3145732
  355.9 6.5 %slice-start = ((s8[5767168]{0:T(1024)(128)(4,1)}), s8[1572864]{0:T(1024)(128)(4,1)S(1)}, s32[]{:S(2)}) async-start(s8[5767168]{0:T(1024)(128)(4,1)} %bitcast.193), calls=%async_computation | async-start | bytes 3145728
  386.9 8.8 %copy-start.22 = (bf16[3,64,1408]{2,1,0:T(8,128)(2,1)S(1)}, bf16[3,64,1408]{2,1,0:T(8,128)(2,1)}, u32[]{:S(2)}) copy-start(bf16[3,64,1408]{2,1,0:T(8,128)(2,1)} %get-tuple-element.96) | copy-start | bytes 1622020
  386.9 9.9 %copy-start.21 = (bf16[3,64,1408]{2,1,0:T(8,128)(2,1)S(1)}, bf16[3,64,1408]{2,1,0:T(8,128)(2,1)}, u32[]{:S(2)}) copy-start(bf16[3,64,1408]{2,1,0:T(8,128)(2,1)} %get-tuple-element.97) | copy-start | bytes 1622020
  401.0 14.6 %copy-start.10 = (bf16[16,11264]{1,0:T(8,128)(2,1)S(1)}, bf16[16,11264]{1,0:T(8,128)(2,1)}, u32[]{:S(2)}) copy-start(bf16[16,11264]{1,0:T(8,128)(2,1)} %param.18) | copy-start | bytes 1081348
  401.0 14.6 %copy-start.39 = (f32[16]{0:T(128)S(1)}, f32[16]{0:T(128)}, u32[]{:S(2)}) copy-start(f32[16]{0:T(128)} %copy-done.38) | copy-start | bytes 196
  415.4 5.7 %copy-start.33 = (bf16[16,2048]{1,0:T(8,128)(2,1)S(1)}, bf16[16,2048]{1,0:T(8,128)(2,1)}, u32[]{:S(2)}) copy-start(bf16[16,2048]{1,0:T(8,128)(2,1)} %get-tuple-element.103) | copy-start | bytes 196612
  415.5 6.4 %copy-start.24 = (bf16[512,8,64]{0,2,1:T(8,128)(2,1)S(1)}, bf16[512,8,64]{0,2,1:T(8,128)(2,1)}, u32[]{:S(2)}) copy-start(bf16[512,8,64]{0,2,1:T(8,128)(2,1)} %pad_maximum_fusion.4) | copy-start | bytes 1572868
  415.5 6.4 %copy-start.32 = (bf16[512,64]{0,1:T(8,128)(2,1)S(1)}, bf16[512,64]{0,1:T(8,128)(2,1)}, u32[]{:S(2)}) copy-start(bf16[512,64]{0,1:T(8,128)(2,1)} %copy-done.31) | copy-start | bytes 196612
  426.8 20.3 %copy-start.5 = (bf16[128,2048]{1,0:T(8,128)(2,1)S(1)}, bf16[128,2048]{1,0:T(8,128)(2,1)}, u32[]{:S(2)}) copy-start(bf16[128,2048]{1,0:T(8,128)(2,1)} %tok_ref.1) | copy-start | bytes 1572868
  426.8 22.1 %copy-start.51 = (bf16[512,1408]{1,0:T(8,128)(2,1)S(1)}, bf16[512,1408]{1,0:T(8,128)(2,1)}, u32[]{:S(2)}) copy-start(bf16[512,1408]{1,0:T(8,128)(2,1)} %get-tuple-element.108) | copy-start | bytes 4325380
  456.2 17.5 %copy-start.3 = (f32[128,2048]{1,0:T(8,128)S(1)}, f32[128,2048]{1,0:T(8,128)}, u32[]{:S(2)}) copy-start(f32[128,2048]{1,0:T(8,128)} %get-tuple-element.69) | copy-start | bytes 3145732
  456.2 17.5 %copy-start.4 = (f32[128,2048]{1,0:T(8,128)S(1)}, f32[128,2048]{1,0:T(8,128)}, u32[]{:S(2)}) copy-start(f32[128,2048]{1,0:T(8,128)} %sum_grad_one.1) | copy-start | bytes 3145732
  456.2 17.5 %copy-start.36 = (f32[128]{0:T(128)S(1)}, f32[128]{0:T(128)}, u32[]{:S(2)}) copy-start(f32[128]{0:T(128)} %copy-done.35) | copy-start | bytes 1540
  456.2 17.5 %copy-start.41 = (f32[128]{0:T(128)S(1)}, f32[128]{0:T(128)}, u32[]{:S(2)}) copy-start(f32[128]{0:T(128)} %copy-done.40) | copy-start | bytes 1540
  (28 other events, 77.6 us)
